TPU v7x, 512 devices: a whole 4x8x8 slice. The times are simulated.
512 devices in a mesh: dp: 32 (over y, x), tensor: 16 (over z, core).
Axes of the slice: x: 4, y: 8, z: 8, core: 2. Of those that a mesh axis runs over, the one named last changes fastest.
Arguments:
- queries: bfloat16 [32, 256, 4096], P('dp', None, 'tensor'), may hold values from -16 to 16
- keys: bfloat16 [128, 192, 4096], P('dp', None, 'tensor'), may hold values from -16 to 16
- values: bfloat16 [128, 192, 4096], P('dp', None, 'tensor'), may hold values from -6 to 6
- cotangent: bfloat16 [32, 256, 4096], P('dp', None, 'tensor'), may hold values from -192 to 192
- passage_ids: int32 [32, 16], replicated, may hold values from 0 to 127, as said below
- store_slot: int32 [128], replicated, may hold values from 0 to 127, as said below
- lengths: int32 [128], replicated, may hold values from 128 to 192
Outputs:
- context: bfloat16 [32, 256, 4096], P('dp', None, 'tensor')
- grad_queries: bfloat16 [32, 256, 4096], P('dp', None, 'tensor')
- grad_keys: bfloat16 [128, 192, 4096], P('dp', None, 'tensor')
- grad_values: bfloat16 [128, 192, 4096], P('dp', None, 'tensor')
- relevance: float32 [128], P('dp')
Inputs may be any that keep to these rules, and one draw needn't show every extreme that they name: `passage_ids`: each row names 16 different passages. No index of dp stores more than 1 passages of one row, and some row has 1 on one index. `store_slot`: A permutation of the storage positions.
All inputs are finite; a program needn't handle non-finite values.
Results may differ from a plain program's by a relative error of at most 0.0019.
The roundings to bfloat16 on the way count: a program that leaves them out, or rounds other values in their place, can miss the bound.
Values may be sent and summed in bfloat16 or wider, within the bound.
A program may use at most 128 MiB of HBM per device.

v0:
```python
import jax
import jax.numpy as jnp
from jax import lax
from jax.sharding import PartitionSpec as P

HD = 64


score_scale = 0.125


def heads_first(stacked, head_count):
    return stacked.reshape(stacked.shape[0], head_count, -1).transpose(1, 0, 2)


def rows_back(stacked):
    return stacked.transpose(1, 0, 2).reshape(stacked.shape[1], -1)


def head_attention(query_head, key_head, value_head, grad_head, live_keys):
    scores = jnp.dot(query_head, key_head.T, preferred_element_type=jnp.float32) * score_scale
    scores = jnp.where(live_keys[None, :], scores, jnp.float32(-1e30))
    row_max = jnp.max(scores, axis=1, keepdims=True)
    raised = jnp.exp(scores - row_max)
    row_sum = jnp.sum(raised, axis=1, keepdims=True)
    attention_prob = raised / row_sum
    attention_low = attention_prob.astype(jnp.bfloat16)
    context = jnp.dot(attention_low, value_head, preferred_element_type=jnp.float32)
    grad_prob = jnp.dot(grad_head, value_head.T, preferred_element_type=jnp.float32)
    row_delta = jnp.sum(attention_prob * grad_prob, axis=1, keepdims=True)
    grad_scores = (attention_prob * (grad_prob - row_delta)).astype(jnp.bfloat16)
    grad_query = jnp.dot(grad_scores, key_head, preferred_element_type=jnp.float32) * score_scale
    key_gradient = (
        jnp.dot(grad_scores.T, query_head, preferred_element_type=jnp.float32) * score_scale
    )
    grad_value = jnp.dot(attention_low.T, grad_head, preferred_element_type=jnp.float32)
    attention_mass = jnp.sum(attention_prob, axis=0)
    log_total = (row_max + jnp.log(row_sum))[:, 0]
    return (
        context,
        grad_query,
        key_gradient,
        grad_value,
        attention_mass,
        log_total,
        row_delta[:, 0],
    )


def local(queries, keys, values, cotangent, passage_ids, store_slot, lengths):
    peer_count = lax.axis_size("dp")
    own_index = lax.axis_index("dp")
    held_count, token_span, features = keys.shape
    question_total, list_size = passage_ids.shape
    passage_total = store_slot.shape[0]
    slot_count = (list_size + peer_count - 1) // peer_count
    local_heads = features // HD
    total_heads = local_heads * lax.axis_size("tensor")
    target_len = queries.shape[1]
    passage_match = (
        passage_ids[:, :, None] == jnp.arange(passage_total, dtype=jnp.int32)[None, None, :]
    ).astype(jnp.int32)
    position = jnp.sum(passage_match * store_slot[None, None, :], axis=2)
    list_length = jnp.sum(passage_match * lengths[None, None, :], axis=2)
    owner_index = position // held_count
    local_row = position % held_count
    mine_flag = (owner_index == own_index).astype(jnp.int32)
    mine_rank = jnp.cumsum(mine_flag, axis=1) - 1
    slot_pick = mine_flag[:, None, :] * (
        mine_rank[:, None, :] == jnp.arange(slot_count, dtype=jnp.int32)[None, :, None]
    ).astype(jnp.int32)
    slot_used = jnp.sum(slot_pick, axis=2)
    slot_local = jnp.sum(slot_pick * local_row[:, None, :], axis=2)
    entry_in_slot = (
        jnp.sum(slot_pick * jnp.arange(list_size, dtype=jnp.int32)[None, None, :], axis=2)
        + slot_used
        - 1
    )
    flat_local = slot_local.reshape(-1)
    send_keys = jnp.take(keys, flat_local, axis=0).reshape(
        peer_count, slot_count, token_span, features
    )
    send_values = jnp.take(values, flat_local, axis=0).reshape(
        peer_count, slot_count, token_span, features
    )
    got_keys, got_values, received_entry = (
        lax.all_to_all(send_keys, "dp", split_axis=0, concat_axis=0, tiled=True),
        lax.all_to_all(send_values, "dp", split_axis=0, concat_axis=0, tiled=True),
        lax.all_to_all(entry_in_slot, "dp", split_axis=0, concat_axis=0, tiled=True),
    )
    flat_entry = received_entry.reshape(-1)
    entry_match = (flat_entry[None, :] == jnp.arange(list_size, dtype=jnp.int32)[:, None]).astype(
        jnp.int32
    )
    source_slot = jnp.sum(
        entry_match * jnp.arange(flat_entry.shape[0], dtype=jnp.int32)[None, :], axis=1
    )
    key_rows = jnp.take(got_keys.reshape(-1, token_span, features), source_slot, axis=0).reshape(
        -1, features
    )
    value_rows = jnp.take(
        got_values.reshape(-1, token_span, features), source_slot, axis=0
    ).reshape(-1, features)
    own_row = (jnp.arange(question_total, dtype=jnp.int32) == own_index).astype(jnp.int32)
    own_length = jnp.sum(list_length * own_row[:, None], axis=0)
    live_keys = (jnp.arange(token_span, dtype=jnp.int32)[None, :] < own_length[:, None]).reshape(-1)
    query_rows = queries[0]
    grad_rows = cotangent[0]
    results = lax.map(
        lambda operands: head_attention(
            operands[0], operands[1], operands[2], operands[3], live_keys
        ),
        (
            heads_first(query_rows, local_heads),
            heads_first(key_rows, local_heads),
            heads_first(value_rows, local_heads),
            heads_first(grad_rows, local_heads),
        ),
    )
    (
        context_heads,
        query_grad_heads,
        key_grad_heads,
        value_grad_heads,
        mass_heads,
        log_heads,
        delta_heads,
    ) = results
    context = rows_back(context_heads).astype(jnp.bfloat16)[None]
    grad_queries = rows_back(query_grad_heads).astype(jnp.bfloat16)[None]
    slot_weight_int = slot_used.reshape(-1)[None, :] * (
        flat_local[None, :] == jnp.arange(held_count, dtype=jnp.int32)[:, None]
    ).astype(jnp.int32)
    weight_per_slot = slot_weight_int.astype(jnp.bfloat16)
    slot_share = slot_weight_int.astype(jnp.float32)
    mass_part = jnp.sum(mass_heads, axis=0).reshape(list_size, token_span).sum(axis=1) / (
        target_len * total_heads
    )
    passage_mass = lax.psum(mass_part, "tensor").astype(jnp.bfloat16)
    back_mass = jnp.dot(
        passage_mass, entry_match.astype(jnp.bfloat16), preferred_element_type=jnp.float32
    )
    back_mass = back_mass.astype(jnp.bfloat16).reshape(peer_count, slot_count)
    back_index = jnp.clip(flat_entry, 0, list_size - 1)
    key_grads = (
        rows_back(key_grad_heads).astype(jnp.bfloat16).reshape(list_size, token_span, features)
    )
    value_grads = (
        rows_back(value_grad_heads).astype(jnp.bfloat16).reshape(list_size, token_span, features)
    )
    back_keys = jnp.take(key_grads, back_index, axis=0).reshape(
        peer_count, slot_count, token_span, features
    )
    back_values = jnp.take(value_grads, back_index, axis=0).reshape(
        peer_count, slot_count, token_span, features
    )
    got_mass = lax.all_to_all(back_mass, "dp", split_axis=0, concat_axis=0, tiled=True)
    fetched_keys, fetched_values = (
        lax.all_to_all(back_keys, "dp", split_axis=0, concat_axis=0, tiled=True),
        lax.all_to_all(back_values, "dp", split_axis=0, concat_axis=0, tiled=True),
    )
    fetched_keys = fetched_keys.reshape(-1, token_span, features)
    fetched_values = fetched_values.reshape(-1, token_span, features)
    returned_mass = got_mass.reshape(-1).astype(jnp.float32)
    grad_keys = jnp.einsum(
        "kz,zfi->kfi", weight_per_slot, fetched_keys, preferred_element_type=jnp.float32
    ).astype(jnp.bfloat16)
    grad_values = jnp.einsum(
        "kz,zfi->kfi", weight_per_slot, fetched_values, preferred_element_type=jnp.float32
    ).astype(jnp.bfloat16)
    relevance = jnp.sum(slot_share * returned_mass[None, :], axis=1)
    return (context, grad_queries, grad_keys, grad_values, relevance)


def solution(mesh):
    in_specs = (
        P("dp", None, "tensor"),
        P("dp", None, "tensor"),
        P("dp", None, "tensor"),
        P("dp", None, "tensor"),
        P(),
        P(),
        P(),
    )
    out_specs = (
        P("dp", None, "tensor"),
        P("dp", None, "tensor"),
        P("dp", None, "tensor"),
        P("dp", None, "tensor"),
        P("dp"),
    )
    return jax.shard_map(local, mesh=mesh, in_specs=in_specs, out_specs=out_specs, check_vma=False)
```

profile of v0, /device:TPU:1, one launch (start us, length us, event | category | flops | bytes accessed | tf_op | source)
XLA Modules:
  0.0 450.8 jit_solution(18045049499192501558)
XLA Ops:
  1.5 1.9 select_reduce_fusion.1
  4.5 10.6 %all-to-all-start.1 = ((s32[32,1,1]{2,1,0:T(1,128)}), s32[32,1,1]{2,1,0:T(1,128)}, u32[]{:S(2)}, u32[]{:S(2)}) async-start(s32[32,1,1]{2,1,0:T(1,128)} %copy.100), calls=%async_computation.1 | async-start | bytes 32768 | tf_op jit(solution)/shard_map/all_to_all | solution.py:89
  15.7 2.4 gather_fusion
  18.1 2.4 gather_fusion.2
  20.6 5.2 %select_bitcast_fusion.2 = (bf16[32,1,192,256]{3,2,1,0:T(8,128)(2,1)}, bf16[32,1,192,256]{3,2,1,0:T(8,128)(2,1)S(1)}) fusion(bf16[32,192,256]{2,1,0:T(8,128)(2,1)} %gather_fusion.2, pred[32]{0:T(512)(128)(4,1)S(1)} %copy-done.21, bf16[32,192,256]{2,1,0:T(8,128)(2,1)} %gather_fusion), kind=kLoop, calls=%fused_computation.58 | loop fusion | flops 3145728 | bytes 12582944 | tf_op jit(solution)/shard_map/reshape | solution.py:83
  25.7 79.6 %all_to_all.35 = bf16[32,1,192,256]{3,2,1,0:T(8,128)(2,1)} all-to-all(bf16[32,1,192,256]{3,2,1,0:T(8,128)(2,1)S(1)} %get-tuple-element.224), channel_id=1, replica_groups=mesh['dp'=32,'tensor'=16] {'dp'}, dimensions={0} | all-to-all | bytes 6291456 | tf_op jit(solution)/shard_map/all_to_all | solution.py:87
  105.4 7.0 %all-to-all-start.2 = ((bf16[32,1,192,256]{3,2,1,0:T(8,128)(2,1)}), bf16[32,1,192,256]{3,2,1,0:T(8,128)(2,1)S(1)}, u32[]{:S(2)}, u32[]{:S(2)}) async-start(bf16[32,1,192,256]{3,2,1,0:T(8,128)(2,1)} %get-tuple-element.223), calls=%async_computation.2 | async-start | bytes 6291456 | tf_op jit(solution)/shard_map/all_to_all | solution.py:88
  114.1 1.4 reduce.4
  115.7 3.7 gather_fusion.1
  119.4 62.5 %all-to-all-done.2 = bf16[32,1,192,256]{3,2,1,0:T(8,128)(2,1)S(1)} async-done(((bf16[32,1,192,256]{3,2,1,0:T(8,128)(2,1)}), bf16[32,1,192,256]{3,2,1,0:T(8,128)(2,1)S(1)}, u32[]{:S(2)}, u32[]{:S(2)}) %all-to-all-start.2) | async-done | bytes 3145760 | tf_op jit(solution)/shard_map/all_to_all | solution.py:88
  181.8 1.8 gather_fusion.3
  183.6 2.2 broadcast_select_fusion
  185.9 3.1 copy.101
  189.0 3.7 reshape_reshape.6
  192.6 3.1 copy.102
  195.7 3.7 reshape_reshape.7
  199.4 27.7 %while.19 = (s32[]{:T(128)}, bf16[4,256,64]{1,2,0:T(8,128)(2,1)}, bf16[4,256,64]{1,2,0:T(8,128)(2,1)}, bf16[4,3072,64]{1,2,0:T(8,128)(2,1)}, bf16[4,3072,64]{1,2...) while((s32[]{:T(128)}, bf16[4,256,64]{1,2,0:T(8,128)(2,1)}, ...), condition=%wide.region_13.16_spmd.clone, body=%wide.region_8.15_spmd.clone.sunk | while | flops 615988480 | bytes 63763872 | solution.py:109
  227.1 4.8 %convert_element_type.124 = bf16[16,192,256]{1,0,2:T(8,128)(2,1)} reshape(bf16[3072,4,64]{0,2,1:T(8,128)(2,1)} %bitcast.159) | data formatting | bytes 3145728 | tf_op jit(solution)/shard_map/convert_element_type | solution.py:146
  232.0 3.5 copy.109
  235.5 3.4 convert_element_type.128
  238.8 3.5 copy.112
  242.3 2.4 gather_fusion.4
  244.7 2.4 gather_fusion.5
  247.4 32.8 %psum.7 = bf16[16]{0:T(256)(128)(2,1)S(1)} all-reduce(f32[16]{0:T(128)S(1)} %broadcast_multiply_fusion), channel_id=1, replica_groups=mesh['dp'=32,'tensor'=16] {'tensor'}, use_global_device_ids=true, to_apply=%region_16.20 | all-reduce | flops 16 | bytes 96 | tf_op jit(solution)/shard_map/psum | solution.py:139
  281.0 5.9 %all-to-all-start.5 = ((bf16[32,1,1]{2,1,0:T(2,128)(2,1)}), bf16[32,1,1]{2,1,0:T(2,128)(2,1)S(1)}, u32[]{:S(2)}, u32[]{:S(2)}) async-start(bf16[32,1,1]{2,1,0:T(2,128)(2,1)} %copy.115), calls=%async_computation.5 | async-start | bytes 32768 | tf_op jit(solution)/shard_map/all_to_all | solution.py:157
  286.9 5.2 %select_bitcast_fusion = (bf16[32,1,192,256]{3,2,1,0:T(8,128)(2,1)S(1)}, bf16[32,1,192,256]{3,2,1,0:T(8,128)(2,1)}) fusion(bf16[32,192,256]{2,1,0:T(8,128)(2,1)} %gather_fusion.5, pred[32]{0:T(512)(128)(4,1)S(1)} %get-tuple-element.214, bf16[32,192,256]{2,1,0:T(8,128)(2,1)} %gather_fusion.4), kind=kLoop, calls=%fused_computation.56 | loop fusion | flops 3145728 | bytes 12582944 | tf_op jit(solution)/shard_map/reshape | solution.py:154
  292.1 3.3 all-to-all-done.5
  295.4 76.3 %all_to_all.36 = bf16[32,1,192,256]{3,2,1,0:T(8,128)(2,1)} all-to-all(bf16[32,1,192,256]{3,2,1,0:T(8,128)(2,1)S(1)} %get-tuple-element.219), channel_id=1, replica_groups=mesh['dp'=32,'tensor'=16] {'dp'}, dimensions={0} | all-to-all | bytes 6291456 | tf_op jit(solution)/shard_map/all_to_all | solution.py:160
  371.8 6.8 %all-to-all-start.3 = ((bf16[32,1,192,256]{3,2,1,0:T(8,128)(2,1)}), bf16[32,1,192,256]{3,2,1,0:T(8,128)(2,1)S(1)}, u32[]{:S(2)}, u32[]{:S(2)}) async-start(bf16[32,1,192,256]{3,2,1,0:T(8,128)(2,1)} %get-tuple-element.220), calls=%async_computation.3 | async-start | bytes 6291456 | tf_op jit(solution)/shard_map/all_to_all | solution.py:159
  381.1 3.8 fusion.45
  385.7 62.5 %all-to-all-done.3 = bf16[32,1,192,256]{3,2,1,0:T(8,128)(2,1)S(1)} async-done(((bf16[32,1,192,256]{3,2,1,0:T(8,128)(2,1)}), bf16[32,1,192,256]{3,2,1,0:T(8,128)(2,1)S(1)}, u32[]{:S(2)}, u32[]{:S(2)}) %all-to-all-start.3) | async-done | bytes 3145760 | tf_op jit(solution)/shard_map/all_to_all | solution.py:159
  448.1 1.8 fusion.42
  (174 shorter events, 36.5 us)
Async XLA Ops:
  0.6 15.0 %copy-start = (bf16[4,192,256]{2,1,0:T(8,128)(2,1)S(1)}, bf16[4,192,256]{2,1,0:T(8,128)(2,1)}, u32[]{:S(2)}) copy-start(bf16[4,192,256]{2,1,0:T(8,128)(2,1)} %param.16) | copy-start | bytes 1179652
  3.8 11.9 %copy-start.17 = (s32[32]{0:T(128)}, s32[32]{0:T(128)S(1)}, u32[]{:S(2)}) copy-start(s32[32]{0:T(128)S(1)} %get-tuple-element.186) | copy-start | bytes 388
  3.8 11.9 %copy-start.19 = (s32[32]{0:T(128)}, s32[32]{0:T(128)S(1)}, u32[]{:S(2)}) copy-start(s32[32]{0:T(128)S(1)} %get-tuple-element.188) | copy-start | bytes 388
  4.5 21.2 %all-to-all-start.1 = ((s32[32,1,1]{2,1,0:T(1,128)}), s32[32,1,1]{2,1,0:T(1,128)}, u32[]{:S(2)}, u32[]{:S(2)}) async-start(s32[32,1,1]{2,1,0:T(1,128)} %copy.100), calls=%async_computation.1 | async-start | bytes 32768 | tf_op jit(solution)/shard_map/all_to_all | solution.py:89
  15.7 2.4 copy-start.2
  18.1 2.5 copy-start.21
  105.4 7.7 %copy-start.8 = (bf16[1,256,256]{2,1,0:T(8,128)(2,1)S(1)}, bf16[1,256,256]{2,1,0:T(8,128)(2,1)}, u32[]{:S(2)}) copy-start(bf16[1,256,256]{2,1,0:T(8,128)(2,1)} %param.15) | copy-start | bytes 393220
  105.4 7.8 %copy-start.9 = (bf16[1,256,256]{2,1,0:T(8,128)(2,1)S(1)}, bf16[1,256,256]{2,1,0:T(8,128)(2,1)}, u32[]{:S(2)}) copy-start(bf16[1,256,256]{2,1,0:T(8,128)(2,1)} %param.18) | copy-start | bytes 393220
  105.4 76.5 %all-to-all-start.2 = ((bf16[32,1,192,256]{3,2,1,0:T(8,128)(2,1)}), bf16[32,1,192,256]{3,2,1,0:T(8,128)(2,1)S(1)}, u32[]{:S(2)}, u32[]{:S(2)}) async-start(bf16[32,1,192,256]{3,2,1,0:T(8,128)(2,1)} %get-tuple-element.223), calls=%async_computation.2 | async-start | bytes 6291456 | tf_op jit(solution)/shard_map/all_to_all | solution.py:88
  192.6 6.8 %copy-start.16 = (f32[4,3072]{1,0:T(4,128)S(1)}, f32[4,3072]{1,0:T(4,128)}, u32[]{:S(2)}) copy-start(f32[4,3072]{1,0:T(4,128)} %custom-call.16) | copy-start | bytes 147460
  202.0 1.8 copy-start.13
  202.7 1.7 copy-start.5
  203.8 1.7 copy-start.4
  208.9 1.4 copy-start.3
  208.9 1.8 copy-start.13
  209.6 1.7 copy-start.5
  210.7 1.7 copy-start.4
  215.8 1.4 copy-start.3
  215.8 1.8 copy-start.13
  216.5 1.7 copy-start.5
  217.6 1.7 copy-start.4
  222.7 1.8 copy-start.13
  223.5 1.7 copy-start.5
  224.6 1.7 copy-start.4
  227.1 8.3 %copy-start.7 = (bf16[4,3072,64]{1,2,0:T(8,128)(2,1)S(1)}, bf16[4,3072,64]{1,2,0:T(8,128)(2,1)}, u32[]{:S(2)}) copy-start(bf16[4,3072,64]{1,2,0:T(8,128)(2,1)} %get-tuple-element.72) | copy-start | bytes 4718596
  281.0 14.4 %all-to-all-start.5 = ((bf16[32,1,1]{2,1,0:T(2,128)(2,1)}), bf16[32,1,1]{2,1,0:T(2,128)(2,1)S(1)}, u32[]{:S(2)}, u32[]{:S(2)}) async-start(bf16[32,1,1]{2,1,0:T(2,128)(2,1)} %copy.115), calls=%async_computation.5 | async-start | bytes 32768 | tf_op jit(solution)/shard_map/all_to_all | solution.py:157
  371.8 6.8 %copy-start.12 = (bf16[4,256,64]{1,2,0:T(8,128)(2,1)S(1)}, bf16[4,256,64]{1,2,0:T(8,128)(2,1)}, u32[]{:S(2)}) copy-start(bf16[4,256,64]{1,2,0:T(8,128)(2,1)} %get-tuple-element.69) | copy-start | bytes 393220
  371.8 7.6 %copy-start.15 = (bf16[4,256,64]{1,2,0:T(8,128)(2,1)S(1)}, bf16[4,256,64]{1,2,0:T(8,128)(2,1)}, u32[]{:S(2)}) copy-start(bf16[4,256,64]{1,2,0:T(8,128)(2,1)} %get-tuple-element.70) | copy-start | bytes 393220
  371.8 8.7 %copy-start.18 = (s32[32]{0:T(128)S(1)}, s32[32]{0:T(128)}, u32[]{:S(2)}) copy-start(s32[32]{0:T(128)} %copy-done.17) | copy-start | bytes 388
  371.8 8.7 %copy-start.20 = (s32[32]{0:T(128)S(1)}, s32[32]{0:T(128)}, u32[]{:S(2)}) copy-start(s32[32]{0:T(128)} %copy-done.19) | copy-start | bytes 388
  371.8 76.3 %all-to-all-start.3 = ((bf16[32,1,192,256]{3,2,1,0:T(8,128)(2,1)}), bf16[32,1,192,256]{3,2,1,0:T(8,128)(2,1)S(1)}, u32[]{:S(2)}, u32[]{:S(2)}) async-start(bf16[32,1,192,256]{3,2,1,0:T(8,128)(2,1)} %get-tuple-element.220), calls=%async_computation.3 | async-start | bytes 6291456 | tf_op jit(solution)/shard_map/all_to_all | solution.py:159
  381.1 69.7 %copy-start.1 = (bf16[4,192,256]{2,1,0:T(8,128)(2,1)S(1)}, bf16[4,192,256]{2,1,0:T(8,128)(2,1)}, u32[]{:S(2)}) copy-start(bf16[4,192,256]{2,1,0:T(8,128)(2,1)} %param.16) | copy-start | bytes 1179652
  (18 other events, 19.2 us)
where the time goes:
time: 455 us; the launch traced here: 451 us
  blocking collectives  189 us (42%)
  waiting for transfers between devices  128 us (28%)
  local copies, waits for them, and re-layouts  56.8 us (12%)
  starting transfers between devices  30.3 us (7%)
  other arithmetic  24.2 us (5%)
  matrix products  20.9 us (5%)
    all_to_all x1, blocking collectives, local(): lax.all_to_all(send_keys, 'dp', split_axis=0, concat_axis=0, tiled=True)  79.6 us
    all_to_all x1, blocking collectives, local(): lax.all_to_all(back_values, 'dp', split_axis=0, concat_axis=0, tiled=True)  76.3 us
    all_to_all x1, waiting for transfers between devices, local(): lax.all_to_all(send_values, 'dp', split_axis=0, concat_axis=0, tiled=True)  62.5 us
    all_to_all x1, waiting for transfers between devices, local(): lax.all_to_all(back_keys, 'dp', split_axis=0, concat_axis=0, tiled=True)  62.5 us
    psum x1, blocking collectives, local(): passage_mass = lax.psum(mass_part, 'tensor').astype(jnp.bfloat16)  32.8 us
    all_to_all x1, starting transfers between devices, local(): lax.all_to_all(entry_in_slot, 'dp', split_axis=0, concat_axis=0, tiled=True)  10.6 us
  transfers between devices with their start and end apart: 4, of which 3 were waited for; matrix products, arithmetic and copies ran while one was open for 7% of the time, Pallas kernels for 0%

commit v1 on v0

v1 whole, which is shorter than its diff:
```python
import jax
import jax.numpy as jnp
from jax import lax
from jax.experimental import pallas as pl
from jax.experimental.pallas import tpu as pltpu
from jax.sharding import PartitionSpec as P

HD = 64
SCALE = 0.125
NEG = -1e30


def dot_nt(a, b):
    return lax.dot_general(a, b, (((1,), (1,)), ((), ())), preferred_element_type=jnp.float32)


def dot_nn(a, b):
    return lax.dot_general(a, b, (((1,), (0,)), ((), ())), preferred_element_type=jnp.float32)


def pass_one(slot_ref, len_ref, q_ref, g_ref, km_ref, vm_ref, st_ref):
    step = pl.program_id(0)
    live_len = len_ref[step]
    heads = km_ref.shape[1]
    rows = km_ref.shape[2]

    @pl.when(live_len == 0)
    def _():
        st_ref[0, 0] = jnp.full(st_ref.shape[2:], NEG, jnp.float32)
        st_ref[0, 1] = jnp.zeros(st_ref.shape[2:], jnp.float32)
        st_ref[0, 2] = jnp.zeros(st_ref.shape[2:], jnp.float32)

    @pl.when(live_len > 0)
    def _():
        slot = slot_ref[step]
        queries = q_ref[0]
        grads = g_ref[0]
        live = lax.broadcasted_iota(jnp.int32, (rows, queries.shape[0]), 0) < live_len
        for h in range(heads):
            scores = dot_nt(km_ref[slot, h], queries) * SCALE
            scores = jnp.where(live, scores, NEG)
            top = jnp.max(scores, axis=0, keepdims=True)
            raised = jnp.exp(scores - top)
            grad_prob = dot_nt(vm_ref[slot, h], grads)
            st_ref[0, 0, h : h + 1] = top
            st_ref[0, 1, h : h + 1] = jnp.sum(raised, axis=0, keepdims=True)
            st_ref[0, 2, h : h + 1] = jnp.sum(raised * grad_prob, axis=0, keepdims=True)


def pick_heads(stacked, lane):
    heads = len(stacked)
    out = stacked[heads - 1]
    for h in range(heads - 2, -1, -1):
        out = jnp.where(lane < (h + 1) * HD, stacked[h], out)
    return out


def pass_two(
    slot_ref, len_ref, q_ref, g_ref, km_ref, vm_ref, kt_ref, vt_ref, fin_ref,
    o_ref, dq_ref, dk_ref, dv_ref, dk_acc, dv_acc,
):
    step = pl.program_id(0)
    live_len = len_ref[step]
    heads = km_ref.shape[1]
    rows = km_ref.shape[2]

    @pl.when(step == 0)
    def _():
        dk_acc[...] = jnp.zeros_like(dk_acc)
        dv_acc[...] = jnp.zeros_like(dv_acc)

    @pl.when(live_len == 0)
    def _():
        o_ref[...] = jnp.zeros_like(o_ref)
        dq_ref[...] = jnp.zeros_like(dq_ref)

    @pl.when(live_len > 0)
    def _():
        slot = slot_ref[step]
        queries = q_ref[0]
        grads = g_ref[0]
        live = lax.broadcasted_iota(jnp.int32, (rows, queries.shape[0]), 0) < live_len
        lane = lax.broadcasted_iota(jnp.int32, (rows, queries.shape[1]), 1)
        dks, dvs = [], []
        for h in range(heads):
            scores = dot_nt(km_ref[slot, h], queries) * SCALE
            prob = jnp.where(live, jnp.exp(scores - fin_ref[0, 0, h : h + 1]), 0.0)
            low = prob.astype(jnp.bfloat16)
            grad_prob = dot_nt(vm_ref[slot, h], grads)
            gs = (prob * (grad_prob - fin_ref[0, 1, h : h + 1])).astype(jnp.bfloat16)
            cut = slice(h * HD, (h + 1) * HD)
            o_ref[0, cut, :] = dot_nn(vt_ref[slot, cut, :], low)
            dq_ref[0, cut, :] = dot_nn(kt_ref[slot, cut, :], gs)
            dks.append(dot_nn(gs, queries))
            dvs.append(dot_nn(low, grads))
        dk = (pick_heads(dks, lane) * SCALE).astype(jnp.bfloat16)
        dv = pick_heads(dvs, lane).astype(jnp.bfloat16)
        dk_acc[slot] += dk.astype(jnp.float32)
        dv_acc[slot] += dv.astype(jnp.float32)

    @pl.when(step == pl.num_programs(0) - 1)
    def _():
        dk_ref[...] = dk_acc[...].astype(jnp.bfloat16)
        dv_ref[...] = dv_acc[...].astype(jnp.bfloat16)


def local(queries, keys, values, cotangent, passage_ids, store_slot, lengths):
    own = lax.axis_index("dp")
    held, rows, feats = keys.shape
    questions = passage_ids.shape[0]
    target = queries.shape[1]
    heads = feats // HD
    total_heads = heads * lax.axis_size("tensor")
    places = own * held + jnp.arange(held, dtype=jnp.int32)
    match = (store_slot[None, :] == places[:, None]).astype(jnp.int32)
    held_id = jnp.sum(match * jnp.arange(store_slot.shape[0], dtype=jnp.int32)[None, :], axis=1)
    held_len = jnp.sum(match * lengths[None, :], axis=1)
    used = jnp.any(passage_ids[:, :, None] == held_id[None, None, :], axis=1).astype(jnp.int32)
    slot = jnp.sum(used * jnp.arange(held, dtype=jnp.int32)[None, :], axis=1)
    live_len = jnp.sum(used * held_len[None, :], axis=1)

    all_q = lax.all_gather(queries[0], "dp")
    all_g = lax.all_gather(cotangent[0], "dp")

    head_of = jnp.arange(feats, dtype=jnp.int32) // HD
    head_mask = head_of[None, :] == jnp.arange(heads, dtype=jnp.int32)[:, None]
    km = jnp.where(head_mask[None, :, None, :], keys[:, None], jnp.bfloat16(0))
    vm = jnp.where(head_mask[None, :, None, :], values[:, None], jnp.bfloat16(0))
    kt = keys.transpose(0, 2, 1)
    vt = values.transpose(0, 2, 1)

    per_q = lambda *rest: pl.BlockSpec((1,) + rest, lambda i, *_: (i,) + (0,) * len(rest))
    whole = lambda a: pl.BlockSpec(a.shape, lambda i, *_: (0,) * a.ndim)
    stats = pl.pallas_call(
        pass_one,
        grid_spec=pltpu.PrefetchScalarGridSpec(
            num_scalar_prefetch=2,
            grid=(questions,),
            in_specs=[per_q(target, feats), per_q(target, feats), whole(km), whole(vm)],
            out_specs=per_q(3, heads, target),
        ),
        out_shape=jax.ShapeDtypeStruct((questions, 3, heads, target), jnp.float32),
        compiler_params=pltpu.CompilerParams(vmem_limit_bytes=40 << 20),
    )(slot, live_len, all_q, all_g, km, vm)

    got = lax.all_to_all(stats, "dp", split_axis=0, concat_axis=0, tiled=True)
    top = jnp.max(got[:, 0], axis=0)
    weight = jnp.exp(got[:, 0] - top[None])
    total = jnp.sum(got[:, 1] * weight, axis=0)
    delta = jnp.sum(got[:, 2] * weight, axis=0) / total
    final = jnp.stack([top + jnp.log(total), delta])
    fin = lax.all_gather(final, "dp")

    out_t = jax.ShapeDtypeStruct((questions, feats, target), jnp.float32)
    o_t, dq_t, dk, dv = pl.pallas_call(
        pass_two,
        grid_spec=pltpu.PrefetchScalarGridSpec(
            num_scalar_prefetch=2,
            grid=(questions,),
            in_specs=[per_q(target, feats), per_q(target, feats), whole(km), whole(vm),
                      whole(kt), whole(vt), per_q(2, heads, target)],
            out_specs=[per_q(feats, target), per_q(feats, target), whole(keys), whole(values)],
            scratch_shapes=[pltpu.VMEM(keys.shape, jnp.float32), pltpu.VMEM(values.shape, jnp.float32)],
        ),
        out_shape=[out_t, out_t, jax.ShapeDtypeStruct(keys.shape, keys.dtype),
                   jax.ShapeDtypeStruct(values.shape, values.dtype)],
        compiler_params=pltpu.CompilerParams(vmem_limit_bytes=48 << 20),
    )(slot, live_len, all_q, all_g, km, vm, kt, vt, fin)

    mass = jnp.sum(stats[:, 1] * jnp.exp(stats[:, 0] - fin[:, 0]), axis=(1, 2)) / (target * total_heads)
    mass = lax.psum(mass, "tensor").astype(jnp.bfloat16).astype(jnp.float32)
    relevance = jnp.sum(used.astype(jnp.float32) * mass[:, None], axis=0)

    o_sum = lax.psum_scatter(o_t, "dp", scatter_dimension=0, tiled=True)
    dq_sum = lax.psum_scatter(dq_t, "dp", scatter_dimension=0, tiled=True)
    context = o_sum.transpose(0, 2, 1).astype(jnp.bfloat16)
    grad_queries = (dq_sum.transpose(0, 2, 1) * SCALE).astype(jnp.bfloat16)
    return context, grad_queries, dk, dv, relevance


def solution(mesh):
    wide = P("dp", None, "tensor")
    return jax.shard_map(
        local,
        mesh=mesh,
        in_specs=(wide, wide, wide, wide, P(), P(), P()),
        out_specs=(wide, wide, wide, wide, P("dp")),
        check_vma=False,
    )
```

time: 455 us -> 808 us (1.78)
  waiting for transfers between devices: 128 us -> 627 us
  blocking collectives: 189 us -> 76.6 us
  Pallas kernels: 0 us -> 60.4 us
  local copies, waits for them, and re-layouts: 56.8 us -> 11 us
  starting transfers between devices: 30.3 us -> 6.24 us
  matrix products: 20.9 us -> 0 us
  other arithmetic: 24.2 us -> 9.07 us
  between operations: 0.96 us -> 13.8 us
    reduce_scatter x0 -> x2, waiting for transfers between devices: none -> 439 us  [the longest x1 236 us: local(): dq_sum = lax.psum_scatter(dq_t, 'dp', scatter_dimension=0, tiled=True)]
    all_gather x0 -> x2, waiting for transfers between devices: none -> 177 us  [the longest x1 89.4 us: local(): all_q = lax.all_gather(queries[0], 'dp')]
    all_to_all x2 -> x0, blocking collectives: 156 us -> none  [the longest x1 79.6 us: local(): lax.all_to_all(send_keys, 'dp', split_axis=0, concat_axis=0, tiled=True)]
    all_to_all x4 -> x1, waiting for transfers between devices: 128 us -> 8.48 us  [local(): got = lax.all_to_all(stats, 'dp', split_axis=0, concat_axis=0, tiled=True)]
    pallas_call x0 -> x2, Pallas kernels: none -> 60.4 us  [the longest x1 43.3 us: local(): pl.pallas_call(pass_two, grid_spec=pltpu.PrefetchScalarGridSpec(num_scala...]
    all_gather x0 -> x1, blocking collectives: none -> 35.2 us  [local(): fin = lax.all_gather(final, 'dp')]
    all_to_all x4 -> x1, starting transfers between devices: 30.3 us -> 6.08 us  [local(): got = lax.all_to_all(stats, 'dp', split_axis=0, concat_axis=0, tiled=True)]
    dot_general x27 -> x0, matrix products: 20.9 us -> none  [the longest x4 4.47 us: head_attention(): jnp.dot(grad_head, value_head.T, preferred_element_type=jnp.float32)]
  transfers between devices with their start and end apart: 4 -> 5, of which waited for: 3 -> 5; matrix products, arithmetic and copies ran while one was open for 7% -> 1% of each run, Pallas kernels for 0% -> 0%
where the time goes in v1:
time: 808 us; the launch traced here: 804 us
  waiting for transfers between devices  627 us (78%)
  blocking collectives  76.6 us (9%)
  Pallas kernels  60.4 us (7%)
  between operations  13.8 us (2%)
  local copies, waits for them, and re-layouts  11 us (1%)
  other arithmetic  9.07 us (1%)
    reduce_scatter x1, waiting for transfers between devices, local(): dq_sum = lax.psum_scatter(dq_t, 'dp', scatter_dimension=0, tiled=True)  236 us
    reduce_scatter x1, waiting for transfers between devices, local(): o_sum = lax.psum_scatter(o_t, 'dp', scatter_dimension=0, tiled=True)  203 us
    all_gather x1, waiting for transfers between devices, local(): all_q = lax.all_gather(queries[0], 'dp')  89.4 us
    all_gather x1, waiting for transfers between devices, local(): all_g = lax.all_gather(cotangent[0], 'dp')  87.8 us
    pallas_call x1, Pallas kernels, local(): pl.pallas_call(pass_two, grid_spec=pltpu.PrefetchScalarGridSpec(num_scala...  43.3 us
    psum x1, blocking collectives, local(): mass = lax.psum(mass, 'tensor').astype(jnp.bfloat16).astype(jnp.float32)  41.4 us
    all_gather x1, blocking collectives, local(): fin = lax.all_gather(final, 'dp')  35.2 us
    pallas_call x1, Pallas kernels, local(): pl.pallas_call(pass_one, grid_spec=pltpu.PrefetchScalarGridSpec(num_scala...  17.1 us
  transfers between devices with their start and end apart: 5, of which 5 were waited for; matrix products, arithmetic and copies ran while one was open for 1% of the time, Pallas kernels for 0%

profile of v1, /device:TPU:1, one launch (start us, length us, event | category | flops | bytes accessed | tf_op | source)
XLA Modules:
  0.0 804.0 jit_solution(10222523843104389393)
XLA Ops:
  7.2 0.7 all-gather.4.cloned.1.call-update
  7.9 0.7 all-gather.6.cloned.1.call-update
  8.7 0.9 fusion.10
  9.6 0.8 compare_reduce_fusion
  10.4 0.1 select_reduce_fusion
  10.4 1.3 broadcast_select_fusion
  11.8 89.4 %all-gather.4.cloned.1.call-done.q_ref = bf16[32,256,256]{2,1,0:T(8,128)(2,1)} async-done(((bf16[1,256,256]{2,1,0:T(8,128)(2,1)}), bf16[32,256,256]{2,1,0:T(8,128)(2,1)}) %all-gather.4.cloned.1.call-update) | async-done | bytes 4194320 | tf_op jit(solution)/shard_map/all_gather | solution.py:122
  101.1 87.8 %all-gather.6.cloned.1.call-done.g_ref = bf16[32,256,256]{2,1,0:T(8,128)(2,1)} async-done(((bf16[1,256,256]{2,1,0:T(8,128)(2,1)}), bf16[32,256,256]{2,1,0:T(8,128)(2,1)}) %all-gather.6.cloned.1.call-update) | async-done | bytes 4194320 | tf_op jit(solution)/shard_map/all_gather | solution.py:123
  188.9 2.2 copy-done
  191.1 2.2 copy-done.1
  193.3 17.1 %shard_map.110 = f32[32,3,4,256]{3,2,1,0:T(4,128)} custom-call(s32[32]{0:T(128)S(1)} %get-tuple-element.33.slot_ref, s32[32]{0:T(128)S(1)} %get-tuple-element.32.len_ref, bf16[32,256,256]{2,1,0:T(8,128)(2,1)S(1)} %copy-done, bf16[32,256,256]{2,1,0:T(8,128)(2,1)S(1)} %copy-done.1, bf16[4,4,192,256]{3,2,1,0:T(8,128)(2,1)S(1)} %get-tuple-element.37.km_ref, ...), custom_call_target="tpu_custom_call" | custom-call | tf_op jit(solution)/shard_map/pallas_call | solution.py:134
  210.4 6.1 all-to-all-start
  216.5 0.0 reduce-scatter.3.cloned.1.call-start
  216.6 1.0 copy.26
  217.6 2.0 copy.27
  219.6 8.5 %all-to-all-done = f32[32,3,4,256]{3,2,1,0:T(4,128)} async-done(((f32[32,3,4,256]{3,2,1,0:T(4,128)}), f32[32,3,4,256]{3,2,1,0:T(4,128)}, u32[]{:S(2)}, u32[]{:S(2)}) %all-to-all-start) | async-done | bytes 393248 | tf_op jit(solution)/shard_map/all_to_all | solution.py:146
  228.1 0.9 bitcast_reduce_fusion
  229.0 1.1 fusion.7
  230.2 35.2 %all-gather = f32[64,4,256]{2,1,0:T(4,128)S(1)} all-gather(f32[2,4,256]{2,1,0:T(4,128)S(1)} %pad_maximum_fusion), channel_id=2, replica_groups=mesh['dp'=32,'tensor'=16] {'dp'}, dimensions={0}, use_global_device_ids=true | all-gather | bytes 270336 | tf_op jit(solution)/shard_map/all_gather | solution.py:152
  265.4 1.0 copy-done.2
  266.5 1.0 copy-done.3
  267.5 43.3 %shard_map.111 = (f32[32,256,256]{2,1,0:T(8,128)}, f32[32,256,256]{2,1,0:T(8,128)}, bf16[4,192,256]{2,1,0:T(8,128)(2,1)}, bf16[4,192,256]{2,1,0:T(8,128)(2,1)}) custom-call(s32[32]{0:T(128)S(1)} %get-tuple-element.33.slot_ref, s32[32]{0:T(128)S(1)} %get-tuple-element.32.len_ref, bf16[32,256,256]{2,1,0:T(8,128)(2,1)} %all-gather.4.cloned.1.call-done.q_ref, ...), custom_call_target="tpu_custom_call" | custom-call | tf_op jit(solution)/shard_map/pallas_call | solution.py:155
  310.9 0.5 reduce-scatter.5.cloned.1.call-update
  311.4 1.3 fusion.3
  312.7 41.4 %psum.7 = bf16[32]{0:T(256)(128)(2,1)S(1)} all-reduce(f32[32]{0:T(128)S(1)} %broadcast_multiply_fusion), channel_id=1, replica_groups=mesh['dp'=32,'tensor'=16] {'tensor'}, use_global_device_ids=true, to_apply=%region_11.12 | all-reduce | flops 32 | bytes 192 | tf_op jit(solution)/shard_map/psum | solution.py:171
  354.1 0.6 multiply_reduce_fusion
  354.7 203.2 %reduce-scatter.3.cloned.1.call-done = f32[1,256,256]{2,1,0:T(8,128)} async-done(((f32[32,256,256]{2,1,0:T(8,128)}), f32[1,256,256]{2,1,0:T(8,128)}) %reduce-scatter.3.cloned.1.call-update) | async-done | bytes 262160 | tf_op jit(solution)/shard_map/reduce_scatter | solution.py:174
  557.9 1.0 convert_bitcast_fusion
  558.9 0.8 copy.30
  559.6 236.1 %reduce-scatter.5.cloned.1.call-done = f32[1,256,256]{2,1,0:T(8,128)} async-done(((f32[32,256,256]{2,1,0:T(8,128)}), f32[1,256,256]{2,1,0:T(8,128)}) %reduce-scatter.5.cloned.1.call-update) | async-done | bytes 262160 | tf_op jit(solution)/shard_map/reduce_scatter | solution.py:175
  795.7 1.0 fusion
  796.7 0.8 copy.31
  (17 shorter events, 0.2 us)
Async XLA Ops:
  7.2 94.0 %all-gather.4.cloned.1.call-start = ((), (), s32[]{:S(2)}) async-start(), calls=%async_computation.3 | async-start | bytes 4325376 | tf_op jit(solution)/shard_map/all_gather | solution.py:122
  7.9 181.0 %all-gather.6.cloned.1.call-start = ((), (), s32[]{:S(2)}) async-start(), calls=%async_computation.4 | async-start | bytes 4325376 | tf_op jit(solution)/shard_map/all_gather | solution.py:123
  188.9 2.2 copy-start
  191.1 2.2 copy-start.1
  193.3 23.3 %copy-start.4 = (bf16[4,192,256]{2,1,0:T(8,128)(2,1)S(1)}, bf16[4,192,256]{2,1,0:T(8,128)(2,1)}, u32[]{:S(2)}) copy-start(bf16[4,192,256]{2,1,0:T(8,128)(2,1)} %param.8) | copy-start | bytes 1179652
  210.4 17.6 %all-to-all-start = ((f32[32,3,4,256]{3,2,1,0:T(4,128)}), f32[32,3,4,256]{3,2,1,0:T(4,128)}, u32[]{:S(2)}, u32[]{:S(2)}) async-start(f32[32,3,4,256]{3,2,1,0:T(4,128)} %shard_map.110), calls=%async_computation | async-start | bytes 786432 | tf_op jit(solution)/shard_map/all_to_all | solution.py:146
  216.5 341.4 %reduce-scatter.3.cloned.1.call-start = ((), (), s32[]{:S(2)}) async-start(), calls=%async_computation.5 | async-start | bytes 8650752 | tf_op jit(solution)/shard_map/reduce_scatter | solution.py:174
  265.4 1.0 copy-start.2
  266.5 1.0 copy-start.3
  310.8 484.9 %reduce-scatter.5.cloned.1.call-start = ((), (), s32[]{:S(2)}) async-start(), calls=%async_computation.6 | async-start | bytes 8650752 | tf_op jit(solution)/shard_map/reduce_scatter | solution.py:175
Sparse Core Ops, SparseCore 0:
  11.2 89.9 all-gather.3
  104.3 84.6 all-gather.5
  310.9 246.8 reduce-scatter.2
  563.0 232.6 reduce-scatter.4

commit v2 on v1

v2 whole, which is shorter than its diff:
```python
import functools

import jax
import jax.numpy as jnp
from jax import lax
from jax.experimental import pallas as pl
from jax.experimental.pallas import tpu as pltpu
from jax.sharding import PartitionSpec as P

HD = 64
SCALE = 0.125
NEG = -1e30
NX = 4
LAG = 2
STEPS = ((1, 0), (-1, 0), (0, 1), (0, -1))


def onward(kind, dy, dx, ny, nx):
    def along(near, size, plus_reach, plus_link):
        links = []
        minus_reach = size - 1 - plus_reach
        gone_plus, gone_minus = (-near) % size, near % size
        if gone_plus < plus_reach:
            links.append(plus_link)
        if gone_minus < minus_reach and (gone_plus == 0 or gone_plus > plus_reach):
            links.append(plus_link + 1)
        return links

    if kind == 0:
        links = along(dx, nx, nx // 2 if dy % 2 == 0 else nx - 1 - nx // 2, 2)
        if dx == 0:
            links += along(dy, ny, ny // 2, 0)
    else:
        links = along(dy, ny, ny // 2 if dx % 2 == 0 else ny - 1 - ny // 2, 0)
        if dx == 0 or dy == 0:
            pass
        if dy == 0:
            links += along(dx, nx, nx - 1 - nx // 2, 2)
    return links


@functools.lru_cache(maxsize=None)
def schedule(ny, nx):
    def moved(link, dy, dx):
        return ((dy - STEPS[link][0]) % ny, (dx - STEPS[link][1]) % nx)

    @functools.lru_cache(maxsize=None)
    def height(kind, dy, dx, link):
        to = moved(link, dy, dx)
        return 1 + max([height(kind, *to, n) for n in onward(kind, *to, ny, nx)], default=0)

    came = {(0, 0, 0): -LAG, (1, 0, 0): -LAG}
    todo = {(k, 0, 0, n) for k in (0, 1) for n in onward(k, 0, 0, ny, nx)}
    slots = []
    while todo:
        t = len(slots)
        now, fresh = [], {}
        for link in range(4):
            able = [j for j in todo if j[3] == link and came[j[:3]] <= t - LAG]
            if able:
                best = max(able, key=lambda j: (height(*j), j))
                todo.remove(best)
                to = moved(link, best[1], best[2])
                now.append((link, best[0], best[1:3], to))
                fresh[(best[0],) + to] = t
        came.update(fresh)
        for k, dy, dx in fresh:
            todo |= {(k, dy, dx, n) for n in onward(k, dy, dx, ny, nx)}
        slots.append(now)
    places = [(dy, dx) for dy in range(ny) for dx in range(nx)]
    ready = {p: max(came[(0,) + p], came[(1,) + p]) for p in places}
    order = sorted(places, key=lambda p: (ready[p], p))
    return slots, order, ready


def dot_nt(a, b):
    return lax.dot_general(a, b, (((1,), (1,)), ((), ())), preferred_element_type=jnp.float32)


def dot_nn(a, b):
    return lax.dot_general(a, b, (((1,), (0,)), ((), ())), preferred_element_type=jnp.float32)


def peer(ny, nx, dy, dx):
    own = lax.axis_index("dp")
    y, x = own // nx, own % nx
    return {"dp": ((y + dy) % ny) * nx + (x + dx) % nx}


def greet(ny, nx, offsets):
    barrier = pltpu.get_barrier_semaphore()
    for off in offsets:
        pl.semaphore_signal(barrier, inc=1, device_id=peer(ny, nx, *off), device_id_type=pl.DeviceIdType.MESH)
    pl.semaphore_wait(barrier, len(offsets))


def gather_kernel(ny, nx, slot_ref, len_ref, q_ref, g_ref, km_ref, vm_ref, aq_ref, ag_ref, st_ref, send_sem, recv_sem):
    slots, order, ready = schedule(ny, nx)
    index = {p: i for i, p in enumerate(order)}
    bufs = (aq_ref, ag_ref)
    count = ny * nx
    rows = km_ref.shape[1] // (km_ref.shape[2] // HD)
    heads = km_ref.shape[2] // HD

    def copies(t):
        out = []
        for link, kind, sent, got in slots[t]:
            out.append(
                pltpu.make_async_remote_copy(
                    src_ref=bufs[kind].at[index[sent]],
                    dst_ref=bufs[kind].at[index[got]],
                    send_sem=send_sem.at[t, link],
                    recv_sem=recv_sem.at[t, link],
                    device_id=peer(ny, nx, *STEPS[link]),
                    device_id_type=pl.DeviceIdType.MESH,
                )
            )
        return out

    def advance(t):
        if t >= LAG:
            for copy in copies(t - LAG):
                copy.wait_recv()
        if t < len(slots):
            for copy in copies(t):
                copy.start()

    aq_ref[0] = q_ref[0]
    ag_ref[0] = g_ref[0]
    greet(ny, nx, STEPS)

    live_row = lax.broadcasted_iota(jnp.int32, (rows, q_ref.shape[1]), 0)

    def body(i, carry):
        passed = 0
        for c in range(count):
            upto = len(slots) + LAG if c == count - 1 else max(passed, ready[order[c]] + LAG + 1)
            if upto > passed:

                @pl.when(i == c)
                def _():
                    for t in range(passed, upto):
                        advance(t)

                passed = upto
        slot = slot_ref[i]
        live = live_row < len_ref[i]
        all_scores = dot_nt(km_ref[slot], aq_ref[i])
        all_grads = dot_nt(vm_ref[slot], ag_ref[i])
        for h in range(heads):
            part = slice(h * rows, (h + 1) * rows)
            scores = jnp.where(live, all_scores[part], NEG)
            top = jnp.max(scores, axis=0, keepdims=True)
            raised = jnp.exp(scores - top)
            st_ref[i, h : h + 1] = top
            st_ref[i, heads + h : heads + h + 1] = jnp.sum(raised, axis=0, keepdims=True)
            st_ref[i, 2 * heads + h : 2 * heads + h + 1] = jnp.sum(raised * all_grads[part], axis=0, keepdims=True)
        return carry

    lax.fori_loop(0, count, body, 0)
    for t in range(len(slots)):
        for copy in copies(t):
            copy.wait_send()


def stats_kernel(ny, nx, st_ref, fin_ref, got, send_sem, recv_sem, send_two, recv_two):
    _, order, _ = schedule(ny, nx)
    index = {p: i for i, p in enumerate(order)}
    heads = st_ref.shape[1] // 3
    greet(ny, nx, order[1:])
    there, back = [], []
    for i, off in enumerate(order[1:], 1):
        there.append(
            pltpu.make_async_remote_copy(
                src_ref=st_ref.at[i], dst_ref=got.at[i], send_sem=send_sem.at[i], recv_sem=recv_sem.at[i],
                device_id=peer(ny, nx, *off), device_id_type=pl.DeviceIdType.MESH,
            )
        )
        mirror = index[((-off[0]) % ny, (-off[1]) % nx)]
        back.append(
            pltpu.make_async_remote_copy(
                src_ref=fin_ref.at[0], dst_ref=fin_ref.at[mirror], send_sem=send_two.at[i], recv_sem=recv_two.at[i],
                device_id=peer(ny, nx, *off), device_id_type=pl.DeviceIdType.MESH,
            )
        )
    for copy in there:
        copy.start()
    got[0] = st_ref[0]
    for copy in there:
        copy.wait_recv()
    tops = got[:, :heads, :]
    top = jnp.max(tops, axis=0)
    weight = jnp.exp(tops - top[None])
    total = jnp.sum(got[:, heads : 2 * heads, :] * weight, axis=0)
    delta = jnp.sum(got[:, 2 * heads :, :] * weight, axis=0) / total
    fin_ref[0, :heads] = top + jnp.log(total)
    fin_ref[0, heads:] = delta
    for copy in back:
        copy.start()
    for copy in back:
        copy.wait_recv()
    for copy in there + back:
        copy.wait_send()


def pick_heads(stacked, lane):
    heads = len(stacked)
    out = stacked[heads - 1]
    for h in range(heads - 2, -1, -1):
        out = jnp.where(lane < (h + 1) * HD, stacked[h], out)
    return out


def reduce_kernel(
    ny, nx, slot_ref, len_ref, aq_ref, ag_ref, km_ref, vm_ref, kt_ref, vt_ref, fin_ref,
    ctx_ref, gq_ref, dk_ref, dv_ref, own_o, own_q, sent_buf, got_buf, dk_acc, dv_acc, send_sem, recv_sem,
):
    slots, order, _ = schedule(ny, nx)
    index = {p: i for i, p in enumerate(order)}
    count = ny * nx
    last = len(slots) - 1
    feats, target = kt_ref.shape[1], aq_ref.shape[1]
    heads = feats // HD
    rows = kt_ref.shape[2]
    held = kt_ref.shape[0]
    owns = (own_o, own_q)
    entries = [(t,) + e for t in range(len(slots)) for e in slots[t]]

    def copy_of(n):
        _, link, _, _, _ = entries[n]
        back = (-STEPS[link][0], -STEPS[link][1])
        return pltpu.make_async_remote_copy(
            src_ref=sent_buf.at[n], dst_ref=got_buf.at[n], send_sem=send_sem.at[n], recv_sem=recv_sem.at[n],
            device_id=peer(ny, nx, *back), device_id_type=pl.DeviceIdType.MESH,
        )

    def children(kind, place):
        return [n for n, (_, _, k, sent, _) in enumerate(entries) if k == kind and sent == place]

    def summed(kind, place):
        kids = children(kind, place)
        for n in kids:
            copy_of(n).wait_recv()
        powers = [jnp.exp2(got_buf[n, feats : feats + 16, :].astype(jnp.float32)) for n in kids]
        for h in range(heads):
            cut = slice(h * HD, (h + 1) * HD)
            acc = owns[kind][index[place], cut, :]
            for n, power in zip(kids, powers):
                acc = acc + got_buf[n, cut, :].astype(jnp.float32) * power[h : h + 1]
            yield cut, acc

    row16 = lax.broadcasted_iota(jnp.int32, (16, target), 0)

    def send_on(n):
        _, _, kind, _, place = entries[n]
        shifts = jnp.zeros((16, target), jnp.float32)
        for h, (cut, acc) in enumerate(summed(kind, place)):
            most = jnp.maximum(jnp.max(jnp.abs(acc), axis=0, keepdims=True), 1e-30)
            shift = jnp.ceil(jnp.log2(most) + 0.01) - 15.0
            coded = jnp.floor(acc * jnp.exp2(-shift) + 0.5)
            sent_buf[n, cut, :] = coded.astype(jnp.int32).astype(jnp.int16)
            shifts = jnp.where(row16 == h, shift, shifts)
        sent_buf[n, feats : feats + 16, :] = shifts.astype(jnp.int32).astype(jnp.int16)
        copy_of(n).start()

    dk_acc[...] = jnp.zeros_like(dk_acc)
    dv_acc[...] = jnp.zeros_like(dv_acc)
    greet(ny, nx, STEPS)

    live_row = lax.broadcasted_iota(jnp.int32, (rows, target), 0)
    lane = lax.broadcasted_iota(jnp.int32, (rows, feats), 1)

    def body(step, carry):
        i = count - 1 - step
        slot = slot_ref[i]
        live = live_row < len_ref[i]
        queries = aq_ref[i]
        grads = ag_ref[i]
        all_scores = dot_nt(km_ref[slot], queries)
        all_grads = dot_nt(vm_ref[slot], grads)
        dks, dvs = [], []
        for h in range(heads):
            part = slice(h * rows, (h + 1) * rows)
            cut = slice(h * HD, (h + 1) * HD)
            prob = jnp.where(live, jnp.exp(all_scores[part] - fin_ref[i, h : h + 1]), 0.0)
            low = prob.astype(jnp.bfloat16)
            gs = (prob * (all_grads[part] - fin_ref[i, heads + h : heads + h + 1])).astype(jnp.bfloat16)
            own_o[i, cut, :] = dot_nn(vt_ref[slot, cut, :], low)
            own_q[i, cut, :] = dot_nn(kt_ref[slot, cut, :], gs)
            dks.append(dot_nn(gs, queries))
            dvs.append(dot_nn(low, grads))
        dk = (pick_heads(dks, lane) * SCALE).astype(jnp.bfloat16).astype(jnp.float32)
        dv = pick_heads(dvs, lane).astype(jnp.bfloat16).astype(jnp.float32)
        for s in range(held):
            mine = jnp.where(slot == s, 1.0, 0.0)
            dk_acc[s] += dk * mine
            dv_acc[s] += dv * mine

        passed = 0
        for c in range(count):
            upto = passed
            while upto <= last and all(index[e[3]] >= count - 1 - c for e in slots[last - upto]):
                upto += 1
            if upto > passed:

                @pl.when(step == c)
                def _():
                    for u in range(passed, upto):
                        for n, e in enumerate(entries):
                            if e[0] == last - u:
                                send_on(n)

                passed = upto
        return carry

    lax.fori_loop(0, count, body, 0)
    dk_ref[...] = dk_acc[...].astype(jnp.bfloat16)
    dv_ref[...] = dv_acc[...].astype(jnp.bfloat16)
    for kind, out, factor in ((0, ctx_ref, 1.0), (1, gq_ref, SCALE)):
        whole = jnp.concatenate([acc for _, acc in summed(kind, (0, 0))], axis=0)
        out[0] = (whole.T * factor).astype(jnp.bfloat16)
    for n in range(len(entries)):
        copy_of(n).wait_send()


def local(queries, keys, values, cotangent, passage_ids, store_slot, lengths):
    own = lax.axis_index("dp")
    count = lax.axis_size("dp")
    nx = NX
    ny = count // nx
    slots, order, _ = schedule(ny, nx)
    entry_count = sum(len(s) for s in slots)
    held, rows, feats = keys.shape
    target = queries.shape[1]
    heads = feats // HD
    total_heads = heads * lax.axis_size("tensor")

    dys = jnp.array([p[0] for p in order], jnp.int32)
    dxs = jnp.array([p[1] for p in order], jnp.int32)
    question = ((own // nx + dys) % ny) * nx + (own % nx + dxs) % nx
    places = own * held + jnp.arange(held, dtype=jnp.int32)
    match = (store_slot[None, :] == places[:, None]).astype(jnp.int32)
    held_id = jnp.sum(match * jnp.arange(store_slot.shape[0], dtype=jnp.int32)[None, :], axis=1)
    held_len = jnp.sum(match * lengths[None, :], axis=1)
    hit = jnp.any(passage_ids[:, :, None] == held_id[None, None, :], axis=1)
    turn = question[:, None] == jnp.arange(count, dtype=jnp.int32)[None, :]
    used = jnp.any(turn[:, :, None] & hit[None, :, :], axis=1).astype(jnp.int32)
    slot = jnp.sum(used * jnp.arange(held, dtype=jnp.int32)[None, :], axis=1)
    live_len = jnp.sum(used * held_len[None, :], axis=1)

    head_of = jnp.arange(feats, dtype=jnp.int32) // HD
    head_mask = (head_of[None, :] == jnp.arange(heads, dtype=jnp.int32)[:, None])[None, :, None, :]
    zero = jnp.bfloat16(0)
    km = jnp.where(head_mask, (keys * jnp.bfloat16(SCALE))[:, None], zero).reshape(held, heads * rows, feats)
    vm = jnp.where(head_mask, values[:, None], zero).reshape(held, heads * rows, feats)
    kt = keys.transpose(0, 2, 1)
    vt = values.transpose(0, 2, 1)

    vmem = pl.BlockSpec(memory_space=pltpu.VMEM)
    smem = pl.BlockSpec(memory_space=pltpu.SMEM)
    dma = pltpu.SemaphoreType.DMA
    gathered = jax.ShapeDtypeStruct((count, target, feats), jnp.bfloat16)
    all_q, all_g, stats = pl.pallas_call(
        functools.partial(gather_kernel, ny, nx),
        in_specs=[smem, smem] + [vmem] * 4,
        out_specs=[vmem] * 3,
        out_shape=[gathered, gathered, jax.ShapeDtypeStruct((count, 3 * heads, target), jnp.float32)],
        scratch_shapes=[dma((len(slots), 4)), dma((len(slots), 4))],
        compiler_params=pltpu.CompilerParams(collective_id=0, has_side_effects=True, vmem_limit_bytes=40 << 20),
    )(slot, live_len, queries, cotangent, km, vm)

    fin = pl.pallas_call(
        functools.partial(stats_kernel, ny, nx),
        in_specs=[vmem],
        out_specs=vmem,
        out_shape=jax.ShapeDtypeStruct((count, 2 * heads, target), jnp.float32),
        scratch_shapes=[pltpu.VMEM((count, 3 * heads, target), jnp.float32)] + [dma((count,))] * 4,
        compiler_params=pltpu.CompilerParams(collective_id=1, has_side_effects=True, vmem_limit_bytes=16 << 20),
    )(stats)

    mass = jnp.sum(stats[:, heads : 2 * heads] * jnp.exp(stats[:, :heads] - fin[:, :heads]), axis=(1, 2))
    mass = lax.psum(mass / (target * total_heads), "tensor").astype(jnp.bfloat16).astype(jnp.float32)
    relevance = jnp.sum(used.astype(jnp.float32) * mass[:, None], axis=0)

    context, grad_queries, grad_keys, grad_values = pl.pallas_call(
        functools.partial(reduce_kernel, ny, nx),
        in_specs=[smem, smem] + [vmem] * 7,
        out_specs=[vmem] * 4,
        out_shape=[jax.ShapeDtypeStruct(a.shape, a.dtype) for a in (queries, queries, keys, values)],
        scratch_shapes=[
            pltpu.VMEM((count, feats, target), jnp.float32),
            pltpu.VMEM((count, feats, target), jnp.float32),
            pltpu.VMEM((entry_count, feats + 16, target), jnp.int16),
            pltpu.VMEM((entry_count, feats + 16, target), jnp.int16),
            pltpu.VMEM(keys.shape, jnp.float32),
            pltpu.VMEM(values.shape, jnp.float32),
            dma((entry_count,)),
            dma((entry_count,)),
        ],
        compiler_params=pltpu.CompilerParams(collective_id=2, has_side_effects=True, vmem_limit_bytes=60 << 20),
    )(slot, live_len, all_q, all_g, km, vm, kt, vt, fin)
    return context, grad_queries, grad_keys, grad_values, relevance


def solution(mesh):
    wide = P("dp", None, "tensor")
    return jax.shard_map(
        local,
        mesh=mesh,
        in_specs=(wide, wide, wide, wide, P(), P(), P()),
        out_specs=(wide, wide, wide, wide, P("dp")),
        check_vma=False,
    )
```

time: 808 us -> 208 us (0.26)
  waiting for transfers between devices: 627 us -> 0 us
  Pallas kernels: 60.4 us -> 152 us
  blocking collectives: 76.6 us -> 37.3 us
  between operations: 13.8 us -> 0.83 us
    reduce_scatter x2 -> x0, waiting for transfers between devices: 439 us -> none  [the longest x1 236 us: local(): dq_sum = lax.psum_scatter(dq_t, 'dp', scatter_dimension=0, tiled=True)]
    all_gather x2 -> x0, waiting for transfers between devices: 177 us -> none  [the longest x1 89.4 us: local(): all_q = lax.all_gather(queries[0], 'dp')]
    pallas_call x2 -> x3, Pallas kernels: 60.4 us -> 152 us  [the longest x1 67.5 us: local(): pl.pallas_call(functools.partial(reduce_kernel, ny, nx), in_specs=[smem,...]
    all_gather x1 -> x0, blocking collectives: 35.2 us -> none  [local(): fin = lax.all_gather(final, 'dp')]
    all_to_all x1 -> x0, waiting for transfers between devices: 8.48 us -> none  [local(): got = lax.all_to_all(stats, 'dp', split_axis=0, concat_axis=0, tiled=True)]
  transfers between devices with their start and end apart: 5 -> 0, of which waited for: 5 -> 0; matrix products, arithmetic and copies ran while one was open for 1% -> 0% of each run, Pallas kernels for 0% -> 0%
where the time goes in v2:
time: 208 us
  Pallas kernels  152 us (73%)
  blocking collectives  37.3 us (18%)
  local copies, waits for them, and re-layouts  11.7 us (6%)
  other arithmetic  6.07 us (3%)
    pallas_call x1, Pallas kernels, local(): pl.pallas_call(functools.partial(reduce_kernel, ny, nx), in_specs=[smem,...  67.5 us
    pallas_call x1, Pallas kernels, local(): pl.pallas_call(functools.partial(gather_kernel, ny, nx), in_specs=[smem,...  58 us
    psum x1, blocking collectives, local(): lax.psum(mass / (target * total_heads), 'tensor').astype(jnp.bfloat16)  37.3 us
    pallas_call x1, Pallas kernels, local(): pl.pallas_call(functools.partial(stats_kernel, ny, nx), in_specs=[vmem],...  26.2 us
    unnamed x30, local copies, waits for them, and re-layouts  11.6 us

profile of v2, /device:TPU:1, one launch (start us, length us, event | category | flops | bytes accessed | tf_op | source)
XLA Modules:
  0.0 207.6 jit_solution(13744180635411177658)
XLA Ops:
  0.7 0.7 fusion.2
  1.3 0.1 iota_compare_fusion
  1.4 0.9 fusion.1
  2.3 0.8 compare_reduce_fusion
  3.1 0.2 and_reduce_fusion
  3.3 0.1 select_reduce_fusion
  3.3 1.0 broadcast_multiply_fusion
  4.4 0.1 broadcast_in_dim.61
  4.5 0.0 copy-start.5
  4.5 0.0 copy-start.6
  4.5 1.4 bitcast_select_fusion
  5.9 0.0 copy-start
  5.9 0.0 copy-start.1
  5.9 0.0 copy-start.9
  5.9 58.0 %shard_map.128 = (bf16[32,256,256]{2,1,0:T(8,128)(2,1)S(1)}, bf16[32,256,256]{2,1,0:T(8,128)(2,1)S(1)}, f32[32,12,256]{2,1,0:T(8,128)S(1)}) custom-call(s32[32]{0:T(128)S(1)} %get-tuple-element.22.slot_ref, s32[32]{0:T(128)S(1)} %get-tuple-element.21.len_ref, bf16[1,256,256]{2,1,0:T(8,128)(2,1)S(1)} %copy-done.5, bf16[1,256,256]{2,1,0:T(8,128)(2,1)S(1)} %copy-done.6, ...), custom_call_target="tpu_custom_call" | custom-call | tf_op jit(solution)/shard_map/pallas_call | solution.py:363
  63.9 1.9 copy-done.2
  65.9 2.0 copy-done.3
  67.8 26.2 %shard_map.129.fin_ref = f32[32,8,256]{2,1,0:T(8,128)S(1)} custom-call(f32[32,12,256]{2,1,0:T(8,128)S(1)} %get-tuple-element.14.st_ref), custom_call_target="tpu_custom_call" | custom-call | tf_op jit(solution)/shard_map/pallas_call | solution.py:372
  94.0 0.0 copy-start.4
  94.0 0.3 multiply_reduce_fusion
  94.4 37.3 %psum.7 = bf16[32]{0:T(256)(128)(2,1)S(1)} all-reduce(f32[32]{0:T(128)S(1)} %broadcast_multiply_fusion.1), channel_id=1, replica_groups=mesh['dp'=32,'tensor'=16] {'tensor'}, use_global_device_ids=true, to_apply=%region_7.8 | all-reduce | flops 32 | bytes 192 | tf_op jit(solution)/shard_map/psum | solution.py:382
  131.7 0.6 multiply_reduce_fusion.1
  132.3 0.0 copy-done.9
  132.4 1.0 copy.17
  133.4 0.0 copy-done.10
  133.4 1.0 copy.18
  134.4 0.0 copy-done.4
  134.4 67.5 %shard_map.130 = (bf16[1,256,256]{2,1,0:T(8,128)(2,1)}, bf16[1,256,256]{2,1,0:T(8,128)(2,1)}, bf16[4,192,256]{2,1,0:T(8,128)(2,1)}, bf16[4,192,256]{2,1,0:T(8,128)(2,1)}) custom-call(s32[32]{0:T(128)} %copy-done.8, s32[32]{0:T(128)} %copy-done.7, bf16[32,256,256]{2,1,0:T(8,128)(2,1)} %copy-done.2, bf16[32,256,256]{2,1,0:T(8,128)(2,1)} %copy-done.3, ...), custom_call_target="tpu_custom_call" | custom-call | tf_op jit(solution)/shard_map/pallas_call | solution.py:385
  201.9 1.6 copy.23
  203.5 1.6 copy.24
  205.1 1.8 copy.25
  206.9 0.7 copy.26
  (18 shorter events, 0.1 us)
Async XLA Ops:
  3.3 2.5 %copy-start.7 = (s32[32]{0:T(128)}, s32[32]{0:T(128)S(1)}, u32[]{:S(2)}) copy-start(s32[32]{0:T(128)S(1)} %get-tuple-element.21.len_ref) | copy-start | bytes 388
  3.3 2.6 %copy-start.8 = (s32[32]{0:T(128)}, s32[32]{0:T(128)S(1)}, u32[]{:S(2)}) copy-start(s32[32]{0:T(128)S(1)} %get-tuple-element.22.slot_ref) | copy-start | bytes 388
  4.5 1.4 copy-start.5
  4.5 1.4 copy-start.6
  5.9 58.1 %copy-start = (bf16[4,768,256]{2,1,0:T(8,128)(2,1)}, bf16[4,768,256]{2,1,0:T(8,128)(2,1)S(1)}, u32[]{:S(2)}) copy-start(bf16[4,768,256]{2,1,0:T(8,128)(2,1)S(1)} %get-tuple-element.23.vm_ref) | copy-start | bytes 4718596
  5.9 58.1 %copy-start.1 = (bf16[4,768,256]{2,1,0:T(8,128)(2,1)}, bf16[4,768,256]{2,1,0:T(8,128)(2,1)S(1)}, u32[]{:S(2)}) copy-start(bf16[4,768,256]{2,1,0:T(8,128)(2,1)S(1)} %get-tuple-element.24.km_ref) | copy-start | bytes 4718596
  5.9 126.4 %copy-start.9 = (bf16[4,192,256]{2,1,0:T(8,128)(2,1)S(1)}, bf16[4,192,256]{2,1,0:T(8,128)(2,1)}, u32[]{:S(2)}) copy-start(bf16[4,192,256]{2,1,0:T(8,128)(2,1)} %param.10) | copy-start | bytes 1179652
  63.9 1.9 copy-start.2
  65.9 2.0 copy-start.3
  67.8 65.5 %copy-start.10 = (bf16[4,192,256]{2,1,0:T(8,128)(2,1)S(1)}, bf16[4,192,256]{2,1,0:T(8,128)(2,1)}, u32[]{:S(2)}) copy-start(bf16[4,192,256]{2,1,0:T(8,128)(2,1)} %param.11) | copy-start | bytes 1179652
  94.0 40.3 %copy-start.4 = (f32[32,8,256]{2,1,0:T(8,128)}, f32[32,8,256]{2,1,0:T(8,128)S(1)}, u32[]{:S(2)}) copy-start(f32[32,8,256]{2,1,0:T(8,128)S(1)} %shard_map.129.fin_ref) | copy-start | bytes 786436
  201.9 5.0 %copy-start.11 = (bf16[4,192,256]{2,1,0:T(8,128)(2,1)S(1)}, bf16[4,192,256]{2,1,0:T(8,128)(2,1)}, u32[]{:S(2)}) copy-start(bf16[4,192,256]{2,1,0:T(8,128)(2,1)} %get-tuple-element.33) | copy-start | bytes 1179652

commit v3 on v2

v3 whole, which is shorter than its diff:
```python
import functools

import jax
import jax.numpy as jnp
from jax import lax
from jax.experimental import pallas as pl
from jax.experimental.pallas import tpu as pltpu
from jax.sharding import PartitionSpec as P

HD = 64
SCALE = 0.125
NEG = -1e30
NX = 4
LAG = 2
STEPS = ((1, 0), (-1, 0), (0, 1), (0, -1))


def onward(kind, dy, dx, ny, nx):
    def along(near, size, plus_reach, plus_link):
        links = []
        minus_reach = size - 1 - plus_reach
        gone_plus, gone_minus = (-near) % size, near % size
        if gone_plus < plus_reach:
            links.append(plus_link)
        if gone_minus < minus_reach and (gone_plus == 0 or gone_plus > plus_reach):
            links.append(plus_link + 1)
        return links

    up = ny // 2
    if kind == 0:
        links = along(dx, nx, nx // 2 if dy % 4 != 3 else nx - 1 - nx // 2, 2)
        if dx == 0:
            links += along(dy, ny, up, 0)
        return links
    far = nx // 2
    plus = up if dx % 2 == 0 else ny - 1 - up
    gone_plus, gone_minus = (-dy) % ny, dy % ny
    near_row = gone_plus <= ny // 4 or gone_minus <= (ny - 1 - up) // 2
    links = along(dy, ny, plus, 0)
    if dx == far:
        links = [n for n in links if (gone_plus < ny // 4 if n == 0 else gone_minus < (ny - 1 - up) // 2)]
    if dy == 0:
        links += along(dx, nx, nx - 1 - far, 2)
    elif dx == far - 1 and not near_row:
        links.append(3)
    return links


@functools.lru_cache(maxsize=None)
def schedule(ny, nx):
    def moved(link, dy, dx):
        return ((dy - STEPS[link][0]) % ny, (dx - STEPS[link][1]) % nx)

    @functools.lru_cache(maxsize=None)
    def height(kind, dy, dx, link):
        to = moved(link, dy, dx)
        return 1 + max([height(kind, *to, n) for n in onward(kind, *to, ny, nx)], default=0)

    came = {(0, 0, 0): -LAG, (1, 0, 0): -LAG}
    todo = {(k, 0, 0, n) for k in (0, 1) for n in onward(k, 0, 0, ny, nx)}
    slots = []
    while todo:
        t = len(slots)
        now, fresh = [], {}
        for link in range(4):
            able = [j for j in todo if j[3] == link and came[j[:3]] <= t - LAG]
            if able:
                best = max(able, key=lambda j: (height(*j), j))
                todo.remove(best)
                to = moved(link, best[1], best[2])
                now.append((link, best[0], best[1:3], to))
                fresh[(best[0],) + to] = t
        came.update(fresh)
        for k, dy, dx in fresh:
            todo |= {(k, dy, dx, n) for n in onward(k, dy, dx, ny, nx)}
        slots.append(now)
    places = [(dy, dx) for dy in range(ny) for dx in range(nx)]
    ready = {p: max(came[(0,) + p], came[(1,) + p]) for p in places}
    order = sorted(places, key=lambda p: (ready[p], p))
    return slots, order, ready


def dot_nt(a, b):
    return lax.dot_general(a, b, (((1,), (1,)), ((), ())), preferred_element_type=jnp.float32)


def dot_nn(a, b):
    return lax.dot_general(a, b, (((1,), (0,)), ((), ())), preferred_element_type=jnp.float32)


def peer(ny, nx, dy, dx):
    own = lax.axis_index("dp")
    y, x = own // nx, own % nx
    return {"dp": ((y + dy) % ny) * nx + (x + dx) % nx}


def remote(src, dst, send_sem, recv_sem, device):
    return pltpu.make_async_remote_copy(
        src_ref=src, dst_ref=dst, send_sem=send_sem, recv_sem=recv_sem,
        device_id=device, device_id_type=pl.DeviceIdType.MESH,
    )


def pick_heads(stacked, lane):
    heads = len(stacked)
    out = stacked[heads - 1]
    for h in range(heads - 2, -1, -1):
        out = jnp.where(lane < (h + 1) * HD, stacked[h], out)
    return out


def merged(parts, heads):
    top = parts[0][:heads]
    for part in parts[1:]:
        top = jnp.maximum(top, part[:heads])
    total = delta = 0.0
    for part in parts:
        weight = jnp.exp(part[:heads] - top)
        total = total + part[heads : 2 * heads] * weight
        delta = delta + part[2 * heads :] * weight
    return top, total, delta


def kernel(
    ny, nx, ranks, slot_ref, len_ref, q_ref, g_ref, k_ref, v_ref,
    ctx_ref, gq_ref, dk_ref, dv_ref, mass_ref,
    aq, ag, km, vm, kt, vt, st, got_x, mid, got_y, fin_x, fin, mass_rows, mass_own, mass_got,
    own_o, own_q, sent_buf, got_buf, dk_acc, dv_acc,
    send_sem, recv_sem, sx_sem, rx_sem, sy_sem, ry_sem, sf_sem, rf_sem, sd_sem, rd_sem, sm_sem, rm_sem, sr_sem, rr_sem,
):
    slots, order, ready = schedule(ny, nx)
    index = {p: i for i, p in enumerate(order)}
    count = ny * nx
    last = len(slots) - 1
    held, rows, feats = k_ref.shape
    target = q_ref.shape[1]
    heads = feats // HD
    rank = lax.axis_index("tensor")
    entries = [(t,) + e for t in range(len(slots)) for e in slots[t]]

    aq[0] = q_ref[0]
    ag[0] = g_ref[0]
    barrier = pltpu.get_barrier_semaphore()
    met = [peer(ny, nx, 0, dx) for dx in range(1, nx)] + [peer(ny, nx, dy, 0) for dy in range(1, ny)]
    met += [{"tensor": lax.rem(rank + r, ranks)} for r in range(1, ranks)]
    for device in met:
        pl.semaphore_signal(barrier, inc=1, device_id=device, device_id_type=pl.DeviceIdType.MESH)
    pl.semaphore_wait(barrier, len(met))

    def gathers(t):
        return [
            remote((aq, ag)[kind].at[index[sent]], (aq, ag)[kind].at[index[got]], send_sem.at[t, link],
                   recv_sem.at[t, link], peer(ny, nx, *STEPS[link]))
            for link, kind, sent, got in slots[t]
        ]

    def advance(t):
        if t >= LAG:
            for copy in gathers(t - LAG):
                copy.wait_recv()
        if t < len(slots):
            for copy in gathers(t):
                copy.start()

    def stat_x(i):
        dy, dx = order[i]
        return remote(st.at[i], got_x.at[dy, (-dx) % nx], sx_sem.at[dy, dx], rx_sem.at[dy, (-dx) % nx], peer(ny, nx, 0, dx))

    first = ready[order[0]] + LAG + 1
    for t in range(first):
        advance(t)

    lane = lax.broadcasted_iota(jnp.int32, (rows, feats), 1)
    for s in range(held):
        keys, values = k_ref[s], v_ref[s]
        kt[s] = keys.astype(jnp.float32).T.astype(jnp.bfloat16)
        vt[s] = values.astype(jnp.float32).T.astype(jnp.bfloat16)
        for h in range(heads):
            mine = (lane >= h * HD) & (lane < (h + 1) * HD)
            km[s, h * rows : (h + 1) * rows] = jnp.where(mine, keys.astype(jnp.float32) * SCALE, 0.0).astype(jnp.bfloat16)
            vm[s, h * rows : (h + 1) * rows] = jnp.where(mine, values.astype(jnp.float32), 0.0).astype(jnp.bfloat16)

    live_row = lax.broadcasted_iota(jnp.int32, (rows, target), 0)

    def pass_one(i, carry):
        passed = first
        for c in range(1, count):
            upto = len(slots) + LAG if c == count - 1 else max(passed, ready[order[c]] + LAG + 1)

            @pl.when(i == c)
            def _():
                for t in range(passed, upto):
                    advance(t)
                if order[c - 1][1]:
                    stat_x(c - 1).start()

            passed = upto
        slot = slot_ref[i]
        live = live_row < len_ref[i]
        all_scores = dot_nt(km[slot], aq[i])
        all_grads = dot_nt(vm[slot], ag[i])
        for h in range(heads):
            part = slice(h * rows, (h + 1) * rows)
            scores = jnp.where(live, all_scores[part], NEG)
            top = jnp.max(scores, axis=0, keepdims=True)
            raised = jnp.exp(scores - top)
            st[i, h : h + 1] = top
            st[i, heads + h : heads + h + 1] = jnp.sum(raised, axis=0, keepdims=True)
            st[i, 2 * heads + h : 2 * heads + h + 1] = jnp.sum(raised * all_grads[part], axis=0, keepdims=True)
        return carry

    lax.fori_loop(0, count, pass_one, 0)
    if order[count - 1][1]:
        stat_x(count - 1).start()

    def stat_y(dy):
        return remote(mid.at[dy], got_y.at[(-dy) % ny], sy_sem.at[dy], ry_sem.at[(-dy) % ny], peer(ny, nx, dy, 0))

    def fin_y(dy):
        return remote(fin_x.at[0, 0], fin_x.at[0, (-dy) % ny], sf_sem.at[dy], rf_sem.at[(-dy) % ny], peer(ny, nx, dy, 0))

    def fin_over_x(dx):
        return remote(fin_x.at[0], fin_x.at[(-dx) % nx], sd_sem.at[dx], rd_sem.at[(-dx) % nx], peer(ny, nx, 0, dx))

    for dy in list(range(1, ny)) + [0]:
        for dx in range(1, nx):
            stat_x(index[(dy, (-dx) % nx)]).wait_recv()
        parts = [st[index[(dy, 0)]]] + [got_x[dy, dx] for dx in range(1, nx)]
        for n, part in enumerate(merged(parts, heads)):
            mid[dy, n * heads : (n + 1) * heads] = part
        if dy:
            stat_y(dy).start()
    for dy in range(1, ny):
        stat_y((-dy) % ny).wait_recv()
    top, total, delta = merged([mid[0]] + [got_y[dy] for dy in range(1, ny)], heads)
    fin_x[0, 0, :heads] = top + jnp.log(total)
    fin_x[0, 0, heads:] = delta / total
    for dy in range(1, ny):
        fin_y(dy).start()
    for dy in range(1, ny):
        fin_y((-dy) % ny).wait_recv()
    for dx in range(1, nx):
        fin_over_x(dx).start()
    for dx in range(1, nx):
        fin_over_x((-dx) % nx).wait_recv()
    for i, (dy, dx) in enumerate(order):
        fin[i] = fin_x[dx, dy]
        share = st[i, heads : 2 * heads] * jnp.exp(st[i, :heads] - fin[i, :heads])
        mass_rows[i : i + 1] = jnp.sum(share, axis=0, keepdims=True)
    mass_own[...] = jnp.broadcast_to(jnp.sum(mass_rows[...], axis=1, keepdims=True), mass_own.shape)

    def masses(r):
        return remote(mass_own, mass_got.at[r], sm_sem.at[r], rm_sem.at[r], {"tensor": lax.rem(rank + r, ranks)})

    for r in range(1, ranks):
        masses(r).start()

    owns = (own_o, own_q)

    def copy_of(n):
        link = entries[n][1]
        return remote(sent_buf.at[n], got_buf.at[n], sr_sem.at[n], rr_sem.at[n], peer(ny, nx, -STEPS[link][0], -STEPS[link][1]))

    def summed(kind, place):
        kids = [n for n, (_, _, k, sent, _) in enumerate(entries) if k == kind and sent == place]
        for n in kids:
            copy_of(n).wait_recv()
        powers = [jnp.exp2(got_buf[n, feats : feats + 16, :].astype(jnp.float32)) for n in kids]
        for h in range(heads):
            cut = slice(h * HD, (h + 1) * HD)
            acc = owns[kind][index[place], cut, :]
            for n, power in zip(kids, powers):
                acc = acc + got_buf[n, cut, :].astype(jnp.float32) * power[h : h + 1]
            yield cut, acc

    row16 = lax.broadcasted_iota(jnp.int32, (16, target), 0)

    def send_on(n):
        _, _, kind, _, place = entries[n]
        shifts = jnp.zeros((16, target), jnp.float32)
        for h, (cut, acc) in enumerate(summed(kind, place)):
            most = jnp.maximum(jnp.max(jnp.abs(acc), axis=0, keepdims=True), 1e-30)
            shift = jnp.ceil(jnp.log2(most) + 0.01) - 15.0
            coded = jnp.floor(acc * jnp.exp2(-shift) + 0.5)
            sent_buf[n, cut, :] = coded.astype(jnp.int32).astype(jnp.int16)
            shifts = jnp.where(row16 == h, shift, shifts)
        sent_buf[n, feats : feats + 16, :] = shifts.astype(jnp.int32).astype(jnp.int16)
        copy_of(n).start()

    dk_acc[...] = jnp.zeros_like(dk_acc)
    dv_acc[...] = jnp.zeros_like(dv_acc)

    def pass_two(step, carry):
        i = count - 1 - step
        slot = slot_ref[i]
        live = live_row < len_ref[i]
        queries = aq[i]
        grads = ag[i]
        all_scores = dot_nt(km[slot], queries)
        all_grads = dot_nt(vm[slot], grads)
        dks, dvs = [], []
        for h in range(heads):
            part = slice(h * rows, (h + 1) * rows)
            cut = slice(h * HD, (h + 1) * HD)
            prob = jnp.where(live, jnp.exp(all_scores[part] - fin[i, h : h + 1]), 0.0)
            low = prob.astype(jnp.bfloat16)
            gs = (prob * (all_grads[part] - fin[i, heads + h : heads + h + 1])).astype(jnp.bfloat16)
            own_o[i, cut, :] = dot_nn(vt[slot, cut, :], low)
            own_q[i, cut, :] = dot_nn(kt[slot, cut, :], gs)
            dks.append(dot_nn(gs, queries))
            dvs.append(dot_nn(low, grads))
        dk = (pick_heads(dks, lane) * SCALE).astype(jnp.bfloat16).astype(jnp.float32)
        dv = pick_heads(dvs, lane).astype(jnp.bfloat16).astype(jnp.float32)
        for s in range(held):
            mine = jnp.where(slot == s, 1.0, 0.0)
            dk_acc[s] += dk * mine
            dv_acc[s] += dv * mine

        passed = 0
        for c in range(count):
            upto = passed
            while upto <= last and all(index[e[3]] >= count - 1 - c for e in slots[last - upto]):
                upto += 1
            if upto > passed:

                @pl.when(step == c)
                def _():
                    for u in range(passed, upto):
                        for n, e in enumerate(entries):
                            if e[0] == last - u:
                                send_on(n)

                passed = upto
        return carry

    lax.fori_loop(0, count, pass_two, 0)
    dk_ref[...] = dk_acc[...].astype(jnp.bfloat16)
    dv_ref[...] = dv_acc[...].astype(jnp.bfloat16)
    mass = mass_own[...]
    for r in range(1, ranks):
        masses(r).wait_recv()
        mass = mass + mass_got[r]
    mass_ref[...] = (mass / (target * heads * ranks)).astype(jnp.bfloat16).astype(jnp.float32)
    for kind, out, factor in ((0, ctx_ref, 1.0), (1, gq_ref, SCALE)):
        whole = jnp.concatenate([acc for _, acc in summed(kind, (0, 0))], axis=0)
        out[0] = (whole.T * factor).astype(jnp.bfloat16)

    for t in range(len(slots)):
        for copy in gathers(t):
            copy.wait_send()
    for i in range(count):
        if order[i][1]:
            stat_x(i).wait_send()
    for dy in range(1, ny):
        stat_y(dy).wait_send()
        fin_y(dy).wait_send()
    for dx in range(1, nx):
        fin_over_x(dx).wait_send()
    for r in range(1, ranks):
        masses(r).wait_send()
    for n in range(len(entries)):
        copy_of(n).wait_send()


def local(queries, keys, values, cotangent, passage_ids, store_slot, lengths):
    own = lax.axis_index("dp")
    count = lax.axis_size("dp")
    nx = NX
    ny = count // nx
    slots, order, _ = schedule(ny, nx)
    entry_count = sum(len(s) for s in slots)
    held, rows, feats = keys.shape
    target = queries.shape[1]
    heads = feats // HD

    dys = jnp.array([p[0] for p in order], jnp.int32)
    dxs = jnp.array([p[1] for p in order], jnp.int32)
    question = ((own // nx + dys) % ny) * nx + (own % nx + dxs) % nx
    places = own * held + jnp.arange(held, dtype=jnp.int32)
    match = (store_slot[None, :] == places[:, None]).astype(jnp.int32)
    held_id = jnp.sum(match * jnp.arange(store_slot.shape[0], dtype=jnp.int32)[None, :], axis=1)
    held_len = jnp.sum(match * lengths[None, :], axis=1)
    hit = jnp.any(passage_ids[:, :, None] == held_id[None, None, :], axis=1)
    turn = question[:, None] == jnp.arange(count, dtype=jnp.int32)[None, :]
    used = jnp.any(turn[:, :, None] & hit[None, :, :], axis=1).astype(jnp.int32)
    slot = jnp.sum(used * jnp.arange(held, dtype=jnp.int32)[None, :], axis=1)
    live_len = jnp.sum(used * held_len[None, :], axis=1)

    vmem = pl.BlockSpec(memory_space=pltpu.VMEM)
    smem = pl.BlockSpec(memory_space=pltpu.SMEM)
    dma = pltpu.SemaphoreType.DMA
    ranks = lax.axis_size("tensor")
    low, full = jnp.bfloat16, jnp.float32
    context, grad_queries, grad_keys, grad_values, mass = pl.pallas_call(
        functools.partial(kernel, ny, nx, ranks),
        in_specs=[smem, smem] + [vmem] * 4,
        out_specs=[vmem] * 5,
        out_shape=[jax.ShapeDtypeStruct(a.shape, a.dtype) for a in (queries, queries, keys, values)]
        + [jax.ShapeDtypeStruct((count, 128), full)],
        scratch_shapes=[
            pltpu.VMEM((count, target, feats), low),
            pltpu.VMEM((count, target, feats), low),
            pltpu.VMEM((held, heads * rows, feats), low),
            pltpu.VMEM((held, heads * rows, feats), low),
            pltpu.VMEM((held, feats, rows), low),
            pltpu.VMEM((held, feats, rows), low),
            pltpu.VMEM((count, 3 * heads, target), full),
            pltpu.VMEM((ny, nx, 3 * heads, target), full),
            pltpu.VMEM((ny, 3 * heads, target), full),
            pltpu.VMEM((ny, 3 * heads, target), full),
            pltpu.VMEM((nx, ny, 2 * heads, target), full),
            pltpu.VMEM((count, 2 * heads, target), full),
            pltpu.VMEM((count, target), full),
            pltpu.VMEM((count, 128), full),
            pltpu.VMEM((ranks, count, 128), full),
            pltpu.VMEM((count, feats, target), full),
            pltpu.VMEM((count, feats, target), full),
            pltpu.VMEM((entry_count, feats + 16, target), jnp.int16),
            pltpu.VMEM((entry_count, feats + 16, target), jnp.int16),
            pltpu.VMEM(keys.shape, full),
            pltpu.VMEM(values.shape, full),
            dma((len(slots), 4)),
            dma((len(slots), 4)),
            dma((ny, nx)),
            dma((ny, nx)),
        ]
        + [dma((ny,))] * 4
        + [dma((nx,))] * 2
        + [dma((ranks,))] * 2
        + [dma((entry_count,))] * 2,
        compiler_params=pltpu.CompilerParams(collective_id=0, has_side_effects=True, vmem_limit_bytes=61 << 20),
    )(slot, live_len, queries, cotangent, keys, values)
    relevance = jnp.sum(used.astype(full) * mass[:, :1], axis=0)
    return context, grad_queries, grad_keys, grad_values, relevance


def solution(mesh):
    wide = P("dp", None, "tensor")
    return jax.shard_map(
        local,
        mesh=mesh,
        in_specs=(wide, wide, wide, wide, P(), P(), P()),
        out_specs=(wide, wide, wide, wide, P("dp")),
        check_vma=False,
    )
```

time: 208 us -> 156 us (0.75)
  the two profiles are of different devices: /device:TPU:1 before, /device:TPU:8 now
where the time goes in v3:
time: 156 us
  Pallas kernels  146 us (94%)
  local copies, waits for them, and re-layouts  7.19 us (5%)
  other arithmetic  1.76 us (1%)
    pallas_call x1, Pallas kernels, local(): pl.pallas_call(functools.partial(kernel, ny, nx, ranks), in_specs=[smem,...  146 us
    unnamed x18, local copies, waits for them, and re-layouts  6.31 us

profile of v3, /device:TPU:8, one launch (start us, length us, event | category | flops | bytes accessed | tf_op | source)
XLA Modules:
  0.0 155.9 jit_solution(8090937205731901553)
XLA Ops:
  0.6 0.0 copy-start.5
  0.7 0.0 copy-start.6
  0.7 0.0 copy-start.2
  0.7 0.6 copy-done.5
  1.3 0.0 copy-done.6
  1.3 0.0 copy-start.3
  1.3 0.0 copy-start.4
  1.3 0.6 copy-done.3
  2.0 0.0 copy-done.4
  2.0 0.2 fusion.1
  2.2 0.0 copy-done.2
  2.2 0.1 compare_reduce_fusion
  2.3 0.1 iota_compare_fusion
  2.3 0.2 and_reduce_fusion
  2.5 0.6 select_reduce_fusion
  3.1 146.2 %shard_map.128 = (bf16[1,256,256]{2,1,0:T(8,128)(2,1)}, bf16[1,256,256]{2,1,0:T(8,128)(2,1)}, bf16[4,192,256]{2,1,0:T(8,128)(2,1)}, bf16[4,192,256]{2,1,0:T(8,128)(2,1)}, f32[32,128]{1,0:T(8,128)}) custom-call(s32[32]{0:T(128)} %get-tuple-element.18.slot_ref, s32[32]{0:T(128)} %get-tuple-element.17.len_ref, bf16[1,256,256]{2,1,0:T(8,128)(2,1)} %q_ref.1, ...), custom_call_target="tpu_custom_call" | custom-call | tf_op jit(solution)/shard_map/pallas_call | solution.py:394
  149.4 0.0 copy-start.1
  149.4 0.9 slice_reduce_fusion
  150.2 0.6 multiply_reduce_fusion
  150.9 1.6 %copy.20 = bf16[1,256,256]{2,1,0:T(8,128)(2,1)} copy(bf16[1,256,256]{2,1,0:T(8,128)(2,1)} %get-tuple-element.24) | data formatting | bytes 262144
  152.4 1.6 %copy.21 = bf16[1,256,256]{2,1,0:T(8,128)(2,1)} copy(bf16[1,256,256]{2,1,0:T(8,128)(2,1)} %get-tuple-element.25) | data formatting | bytes 262144
  154.0 0.0 copy-done.1
  154.0 0.0 copy-start
  154.0 0.7 copy.22
  154.8 0.4 copy-done
  155.2 0.7 copy.23
  (2 shorter events, 0.0 us)
Async XLA Ops:
  0.6 0.7 copy-start.5
  0.7 0.7 copy-start.6
  0.7 1.5 copy-start.2
  1.3 0.7 copy-start.3
  1.3 0.7 copy-start.4
  149.4 4.7 %copy-start.1 = (bf16[4,192,256]{2,1,0:T(8,128)(2,1)S(1)}, bf16[4,192,256]{2,1,0:T(8,128)(2,1)}, u32[]{:S(2)}) copy-start(bf16[4,192,256]{2,1,0:T(8,128)(2,1)} %get-tuple-element.26) | copy-start | bytes 1179652
  154.0 1.1 copy-start

commit v4 on v3

--- a/solution.py
+++ b/solution.py
@@ -109,37 +109,37 @@
     return out
 
 
-def merged(parts, heads):
-    top = parts[0][:heads]
-    for part in parts[1:]:
-        top = jnp.maximum(top, part[:heads])
-    total = delta = 0.0
-    for part in parts:
-        weight = jnp.exp(part[:heads] - top)
-        total = total + part[heads : 2 * heads] * weight
-        delta = delta + part[2 * heads :] * weight
+def merged(got, lines):
+    top = jnp.max(got[..., :lines, :], axis=0)
+    weight = jnp.exp(got[..., :lines, :] - top[None])
+    total = jnp.sum(got[..., lines : 2 * lines, :] * weight, axis=0)
+    delta = jnp.sum(got[..., 2 * lines :, :] * weight, axis=0)
     return top, total, delta
 
 
 def kernel(
     ny, nx, ranks, slot_ref, len_ref, q_ref, g_ref, k_ref, v_ref,
     ctx_ref, gq_ref, dk_ref, dv_ref, mass_ref,
-    aq, ag, km, vm, kt, vt, st, got_x, mid, got_y, fin_x, fin, mass_rows, mass_own, mass_got,
+    aq, ag, km, vm, kt, vt, st, got_x, mid, got_y, fin_x, fin, mass_own, mass_got,
     own_o, own_q, sent_buf, got_buf, dk_acc, dv_acc,
     send_sem, recv_sem, sx_sem, rx_sem, sy_sem, ry_sem, sf_sem, rf_sem, sd_sem, rd_sem, sm_sem, rm_sem, sr_sem, rr_sem,
 ):
     slots, order, ready = schedule(ny, nx)
     index = {p: i for i, p in enumerate(order)}
     count = ny * nx
-    last = len(slots) - 1
-    held, rows, feats = k_ref.shape
+    length = len(slots)
+    held, rows, _ = k_ref.shape
     target = q_ref.shape[1]
-    heads = feats // HD
+    width = aq.shape[2]
+    heads = width // HD
+    wraps = target // 128
+    lines = heads * wraps
     rank = lax.axis_index("tensor")
-    entries = [(t,) + e for t in range(len(slots)) for e in slots[t]]
+    entries = [(t,) + e for t in range(length) for e in slots[t]]
 
     aq[0] = q_ref[0]
     ag[0] = g_ref[0]
+
     barrier = pltpu.get_barrier_semaphore()
     met = [peer(ny, nx, 0, dx) for dx in range(1, nx)] + [peer(ny, nx, dy, 0) for dy in range(1, ny)]
     met += [{"tensor": lax.rem(rank + r, ranks)} for r in range(1, ranks)]
@@ -147,50 +147,98 @@
         pl.semaphore_signal(barrier, inc=1, device_id=device, device_id_type=pl.DeviceIdType.MESH)
     pl.semaphore_wait(barrier, len(met))
 
-    def gathers(t):
+    def gathers(g):
         return [
-            remote((aq, ag)[kind].at[index[sent]], (aq, ag)[kind].at[index[got]], send_sem.at[t, link],
-                   recv_sem.at[t, link], peer(ny, nx, *STEPS[link]))
-            for link, kind, sent, got in slots[t]
+            remote((aq, ag)[kind].at[index[sent]], (aq, ag)[kind].at[index[got]], send_sem.at[g, link],
+                   recv_sem.at[g, link], peer(ny, nx, *STEPS[link]))
+            for link, kind, sent, got in slots[g]
         ]
 
-    def advance(t):
-        if t >= LAG:
-            for copy in gathers(t - LAG):
+    def advance(g):
+        if g >= LAG:
+            for copy in gathers(g - LAG):
                 copy.wait_recv()
-        if t < len(slots):
-            for copy in gathers(t):
+        if g < length:
+            for copy in gathers(g):
                 copy.start()
 
     def stat_x(i):
         dy, dx = order[i]
-        return remote(st.at[i], got_x.at[dy, (-dx) % nx], sx_sem.at[dy, dx], rx_sem.at[dy, (-dx) % nx], peer(ny, nx, 0, dx))
-
-    first = ready[order[0]] + LAG + 1
-    for t in range(first):
-        advance(t)
-
-    lane = lax.broadcasted_iota(jnp.int32, (rows, feats), 1)
+        back = (-dx) % nx
+        return remote(st.at[i], got_x.at[back, dy], sx_sem.at[dy, dx], rx_sem.at[dy, back], peer(ny, nx, 0, dx))
+
+    def stat_y(dy):
+        back = (-dy) % ny
+        return remote(mid.at[dy], got_y.at[back], sy_sem.at[dy], ry_sem.at[back], peer(ny, nx, dy, 0))
+
+    def fin_y(dy):
+        back = (-dy) % ny
+        return remote(fin_x.at[0, 0], fin_x.at[0, back], sf_sem.at[dy], rf_sem.at[back], peer(ny, nx, dy, 0))
+
+    def fin_over_x(dy, dx):
+        back = (-dx) % nx
+        return remote(fin_x.at[0, dy], fin_x.at[back, dy], sd_sem.at[dy, dx], rd_sem.at[dy, back], peer(ny, nx, 0, dx))
+
+    def stage(n):
+        if n == 0:
+            for i in range(count):
+                if order[i][1]:
+                    stat_x(i).wait_recv()
+                else:
+                    got_x[0, order[i][0]] = st[i]
+            for k, stat in enumerate(merged(got_x[...], lines)):
+                mid[:, k * lines : (k + 1) * lines] = stat
+            for dy in range(1, ny):
+                stat_y(dy).start()
+            got_y[0] = mid[0]
+        elif n == 1:
+            for dy in range(1, ny):
+                stat_y(dy).wait_recv()
+            top, total, delta = merged(got_y[...], lines)
+            fin_x[0, 0, :lines] = top + jnp.log(total)
+            fin_x[0, 0, lines:] = delta / total
+            for dy in range(1, ny):
+                fin_y(dy).start()
+            for dx in range(1, nx):
+                fin_over_x(0, dx).start()
+        elif n == 2:
+            for dy in sorted(range(1, ny), key=lambda d: min(d, ny - d)):
+                fin_y(-dy % ny).wait_recv()
+                for dx in range(1, nx):
+                    fin_over_x(dy, dx).start()
+        else:
+            for dx in range(1, nx):
+                for dy in range(ny):
+                    fin_over_x(dy, dx).wait_recv()
+            for i, (dy, dx) in enumerate(order):
+                fin[i] = fin_x[dx, dy]
+
+    for g in range(LAG):
+        advance(g)
+
+    lane = lax.broadcasted_iota(jnp.int32, (rows, width), 1)
     for s in range(held):
-        keys, values = k_ref[s], v_ref[s]
-        kt[s] = keys.astype(jnp.float32).T.astype(jnp.bfloat16)
-        vt[s] = values.astype(jnp.float32).T.astype(jnp.bfloat16)
+        keys, values = k_ref[s].astype(jnp.float32), v_ref[s].astype(jnp.float32)
+        kt[s] = keys.T.astype(jnp.bfloat16)
+        vt[s] = values.T.astype(jnp.bfloat16)
         for h in range(heads):
             mine = (lane >= h * HD) & (lane < (h + 1) * HD)
-            km[s, h * rows : (h + 1) * rows] = jnp.where(mine, keys.astype(jnp.float32) * SCALE, 0.0).astype(jnp.bfloat16)
-            vm[s, h * rows : (h + 1) * rows] = jnp.where(mine, values.astype(jnp.float32), 0.0).astype(jnp.bfloat16)
+            km[s, h * rows : (h + 1) * rows] = jnp.where(mine, keys * SCALE, 0.0).astype(jnp.bfloat16)
+            vm[s, h * rows : (h + 1) * rows] = jnp.where(mine, values, 0.0).astype(jnp.bfloat16)
 
     live_row = lax.broadcasted_iota(jnp.int32, (rows, target), 0)
 
     def pass_one(i, carry):
-        passed = first
+        passed = LAG
         for c in range(1, count):
-            upto = len(slots) + LAG if c == count - 1 else max(passed, ready[order[c]] + LAG + 1)
+            upto = max(passed, ready[order[c]] + LAG + 1)
+            if c == count - 1:
+                upto = length + LAG
 
             @pl.when(i == c)
             def _():
-                for t in range(passed, upto):
-                    advance(t)
+                for g in range(passed, upto):
+                    advance(g)
                 if order[c - 1][1]:
                     stat_x(c - 1).start()
 
@@ -200,54 +248,28 @@
         all_scores = dot_nt(km[slot], aq[i])
         all_grads = dot_nt(vm[slot], ag[i])
         for h in range(heads):
-            part = slice(h * rows, (h + 1) * rows)
-            scores = jnp.where(live, all_scores[part], NEG)
+            cut = slice(h * rows, (h + 1) * rows)
+            scores = jnp.where(live, all_scores[cut], NEG)
             top = jnp.max(scores, axis=0, keepdims=True)
             raised = jnp.exp(scores - top)
-            st[i, h : h + 1] = top
-            st[i, heads + h : heads + h + 1] = jnp.sum(raised, axis=0, keepdims=True)
-            st[i, 2 * heads + h : 2 * heads + h + 1] = jnp.sum(raised * all_grads[part], axis=0, keepdims=True)
+            total = jnp.sum(raised, axis=0, keepdims=True)
+            delta = jnp.sum(raised * all_grads[cut], axis=0, keepdims=True)
+            for k, stat in enumerate((top, total, delta)):
+                for w in range(wraps):
+                    line = k * lines + h * wraps + w
+                    st[i, line : line + 1] = stat[:, w * 128 : (w + 1) * 128]
         return carry
 
     lax.fori_loop(0, count, pass_one, 0)
     if order[count - 1][1]:
         stat_x(count - 1).start()
-
-    def stat_y(dy):
-        return remote(mid.at[dy], got_y.at[(-dy) % ny], sy_sem.at[dy], ry_sem.at[(-dy) % ny], peer(ny, nx, dy, 0))
-
-    def fin_y(dy):
-        return remote(fin_x.at[0, 0], fin_x.at[0, (-dy) % ny], sf_sem.at[dy], rf_sem.at[(-dy) % ny], peer(ny, nx, dy, 0))
-
-    def fin_over_x(dx):
-        return remote(fin_x.at[0], fin_x.at[(-dx) % nx], sd_sem.at[dx], rd_sem.at[(-dx) % nx], peer(ny, nx, 0, dx))
-
-    for dy in list(range(1, ny)) + [0]:
-        for dx in range(1, nx):
-            stat_x(index[(dy, (-dx) % nx)]).wait_recv()
-        parts = [st[index[(dy, 0)]]] + [got_x[dy, dx] for dx in range(1, nx)]
-        for n, part in enumerate(merged(parts, heads)):
-            mid[dy, n * heads : (n + 1) * heads] = part
-        if dy:
-            stat_y(dy).start()
-    for dy in range(1, ny):
-        stat_y((-dy) % ny).wait_recv()
-    top, total, delta = merged([mid[0]] + [got_y[dy] for dy in range(1, ny)], heads)
-    fin_x[0, 0, :heads] = top + jnp.log(total)
-    fin_x[0, 0, heads:] = delta / total
-    for dy in range(1, ny):
-        fin_y(dy).start()
-    for dy in range(1, ny):
-        fin_y((-dy) % ny).wait_recv()
-    for dx in range(1, nx):
-        fin_over_x(dx).start()
-    for dx in range(1, nx):
-        fin_over_x((-dx) % nx).wait_recv()
-    for i, (dy, dx) in enumerate(order):
-        fin[i] = fin_x[dx, dy]
-        share = st[i, heads : 2 * heads] * jnp.exp(st[i, :heads] - fin[i, :heads])
-        mass_rows[i : i + 1] = jnp.sum(share, axis=0, keepdims=True)
-    mass_own[...] = jnp.broadcast_to(jnp.sum(mass_rows[...], axis=1, keepdims=True), mass_own.shape)
+    for n in range(4):
+        stage(n)
+
+    share = jnp.sum(st[:, lines : 2 * lines] * jnp.exp(st[:, :lines] - fin[:, :lines]), axis=1)
+    per_row = jnp.sum(share, axis=1, keepdims=True)
+    diagonal = lax.broadcasted_iota(jnp.int32, (count, 128), 0) == lax.broadcasted_iota(jnp.int32, (count, 128), 1)
+    mass_own[...] = jnp.broadcast_to(jnp.sum(jnp.where(diagonal, per_row, 0.0), axis=0, keepdims=True), mass_own.shape)
 
     def masses(r):
         return remote(mass_own, mass_got.at[r], sm_sem.at[r], rm_sem.at[r], {"tensor": lax.rem(rank + r, ranks)})
@@ -265,7 +287,7 @@
         kids = [n for n, (_, _, k, sent, _) in enumerate(entries) if k == kind and sent == place]
         for n in kids:
             copy_of(n).wait_recv()
-        powers = [jnp.exp2(got_buf[n, feats : feats + 16, :].astype(jnp.float32)) for n in kids]
+        powers = [jnp.exp2(got_buf[n, width : width + 16, :].astype(jnp.float32)) for n in kids]
         for h in range(heads):
             cut = slice(h * HD, (h + 1) * HD)
             acc = owns[kind][index[place], cut, :]
@@ -284,7 +306,7 @@
             coded = jnp.floor(acc * jnp.exp2(-shift) + 0.5)
             sent_buf[n, cut, :] = coded.astype(jnp.int32).astype(jnp.int16)
             shifts = jnp.where(row16 == h, shift, shifts)
-        sent_buf[n, feats : feats + 16, :] = shifts.astype(jnp.int32).astype(jnp.int16)
+        sent_buf[n, width : width + 16, :] = shifts.astype(jnp.int32).astype(jnp.int16)
         copy_of(n).start()
 
     dk_acc[...] = jnp.zeros_like(dk_acc)
@@ -300,11 +322,14 @@
         all_grads = dot_nt(vm[slot], grads)
         dks, dvs = [], []
         for h in range(heads):
-            part = slice(h * rows, (h + 1) * rows)
             cut = slice(h * HD, (h + 1) * HD)
-            prob = jnp.where(live, jnp.exp(all_scores[part] - fin[i, h : h + 1]), 0.0)
+            log_sum, delta = [
+                jnp.concatenate([fin[i, k * lines + h * wraps + w][None] for w in range(wraps)], axis=1)
+                for k in range(2)
+            ]
+            prob = jnp.where(live, jnp.exp(all_scores[h * rows : (h + 1) * rows] - log_sum), 0.0)
             low = prob.astype(jnp.bfloat16)
-            gs = (prob * (all_grads[part] - fin[i, heads + h : heads + h + 1])).astype(jnp.bfloat16)
+            gs = (prob * (all_grads[h * rows : (h + 1) * rows] - delta)).astype(jnp.bfloat16)
             own_o[i, cut, :] = dot_nn(vt[slot, cut, :], low)
             own_q[i, cut, :] = dot_nn(kt[slot, cut, :], gs)
             dks.append(dot_nn(gs, queries))
@@ -319,7 +344,7 @@
         passed = 0
         for c in range(count):
             upto = passed
-            while upto <= last and all(index[e[3]] >= count - 1 - c for e in slots[last - upto]):
+            while upto < length and all(index[e[3]] >= count - 1 - c for e in slots[length - 1 - upto]):
                 upto += 1
             if upto > passed:
 
@@ -327,39 +352,46 @@
                 def _():
                     for u in range(passed, upto):
                         for n, e in enumerate(entries):
-                            if e[0] == last - u:
+                            if e[0] == length - 1 - u:
                                 send_on(n)
 
                 passed = upto
         return carry
 
     lax.fori_loop(0, count, pass_two, 0)
+
     dk_ref[...] = dk_acc[...].astype(jnp.bfloat16)
     dv_ref[...] = dv_acc[...].astype(jnp.bfloat16)
+    for kind, out, factor in ((0, ctx_ref, 1.0), (1, gq_ref, SCALE)):
+        whole = jnp.concatenate([acc for _, acc in summed(kind, (0, 0))], axis=0)
+        out[0] = (whole.T * factor).astype(jnp.bfloat16)
     mass = mass_own[...]
     for r in range(1, ranks):
         masses(r).wait_recv()
         mass = mass + mass_got[r]
     mass_ref[...] = (mass / (target * heads * ranks)).astype(jnp.bfloat16).astype(jnp.float32)
-    for kind, out, factor in ((0, ctx_ref, 1.0), (1, gq_ref, SCALE)):
-        whole = jnp.concatenate([acc for _, acc in summed(kind, (0, 0))], axis=0)
-        out[0] = (whole.T * factor).astype(jnp.bfloat16)
-
-    for t in range(len(slots)):
-        for copy in gathers(t):
+
+    for g in range(length):
+        for copy in gathers(g):
             copy.wait_send()
+    for r in range(1, ranks):
+        masses(r).wait_send()
     for i in range(count):
         if order[i][1]:
             stat_x(i).wait_send()
-    for dy in range(1, ny):
-        stat_y(dy).wait_send()
-        fin_y(dy).wait_send()
-    for dx in range(1, nx):
-        fin_over_x(dx).wait_send()
-    for r in range(1, ranks):
-        masses(r).wait_send()
+    for dy in range(ny):
+        if dy:
+            stat_y(dy).wait_send()
+            fin_y(dy).wait_send()
+        for dx in range(1, nx):
+            fin_over_x(dy, dx).wait_send()
     for n in range(len(entries)):
         copy_of(n).wait_send()
+
+
+def hand_over(*refs):
+    for n in range(len(refs) // 2):
+        refs[len(refs) // 2 + n][...] = refs[n][...]
 
 
 def local(queries, keys, values, cotangent, passage_ids, store_slot, lengths):
@@ -391,12 +423,14 @@
     dma = pltpu.SemaphoreType.DMA
     ranks = lax.axis_size("tensor")
     low, full = jnp.bfloat16, jnp.float32
-    context, grad_queries, grad_keys, grad_values, mass = pl.pallas_call(
+    heads = feats // HD
+    lines = heads * target // 128
+    outs = [jax.ShapeDtypeStruct(a.shape, a.dtype) for a in (queries, queries, keys, values)]
+    *results, mass = pl.pallas_call(
         functools.partial(kernel, ny, nx, ranks),
         in_specs=[smem, smem] + [vmem] * 4,
         out_specs=[vmem] * 5,
-        out_shape=[jax.ShapeDtypeStruct(a.shape, a.dtype) for a in (queries, queries, keys, values)]
-        + [jax.ShapeDtypeStruct((count, 128), full)],
+        out_shape=outs + [jax.ShapeDtypeStruct((8, 128), full)],
         scratch_shapes=[
             pltpu.VMEM((count, target, feats), low),
             pltpu.VMEM((count, target, feats), low),
@@ -404,33 +438,39 @@
             pltpu.VMEM((held, heads * rows, feats), low),
             pltpu.VMEM((held, feats, rows), low),
             pltpu.VMEM((held, feats, rows), low),
-            pltpu.VMEM((count, 3 * heads, target), full),
-            pltpu.VMEM((ny, nx, 3 * heads, target), full),
-            pltpu.VMEM((ny, 3 * heads, target), full),
-            pltpu.VMEM((ny, 3 * heads, target), full),
-            pltpu.VMEM((nx, ny, 2 * heads, target), full),
-            pltpu.VMEM((count, 2 * heads, target), full),
-            pltpu.VMEM((count, target), full),
-            pltpu.VMEM((count, 128), full),
-            pltpu.VMEM((ranks, count, 128), full),
+            pltpu.VMEM((count, 3 * lines, 128), full),
+            pltpu.VMEM((nx, ny, 3 * lines, 128), full),
+            pltpu.VMEM((ny, 3 * lines, 128), full),
+            pltpu.VMEM((ny, 3 * lines, 128), full),
+            pltpu.VMEM((nx, ny, 2 * lines, 128), full),
+            pltpu.VMEM((count, 2 * lines, 128), full),
+            pltpu.VMEM((8, 128), full),
+            pltpu.VMEM((ranks, 8, 128), full),
             pltpu.VMEM((count, feats, target), full),
             pltpu.VMEM((count, feats, target), full),
             pltpu.VMEM((entry_count, feats + 16, target), jnp.int16),
             pltpu.VMEM((entry_count, feats + 16, target), jnp.int16),
-            pltpu.VMEM(keys.shape, full),
-            pltpu.VMEM(values.shape, full),
+            pltpu.VMEM((held, rows, feats), full),
+            pltpu.VMEM((held, rows, feats), full),
             dma((len(slots), 4)),
             dma((len(slots), 4)),
             dma((ny, nx)),
             dma((ny, nx)),
         ]
         + [dma((ny,))] * 4
-        + [dma((nx,))] * 2
+        + [dma((ny, nx))] * 2
         + [dma((ranks,))] * 2
         + [dma((entry_count,))] * 2,
-        compiler_params=pltpu.CompilerParams(collective_id=0, has_side_effects=True, vmem_limit_bytes=61 << 20),
+        compiler_params=pltpu.CompilerParams(collective_id=0, has_side_effects=True, vmem_limit_bytes=62 << 20),
     )(slot, live_len, queries, cotangent, keys, values)
-    relevance = jnp.sum(used.astype(full) * mass[:, :1], axis=0)
+    context, grad_queries, grad_keys, grad_values = pl.pallas_call(
+        hand_over,
+        in_specs=[vmem] * 4,
+        out_specs=[vmem] * 4,
+        out_shape=outs,
+        compiler_params=pltpu.CompilerParams(vmem_limit_bytes=16 << 20),
+    )(*results)
+    relevance = jnp.sum(used.astype(full) * mass[0, :count, None], axis=0)
     return context, grad_queries, grad_keys, grad_values, relevance
 
 

time: 156 us -> 156 us (level)
  no operation moved by 1% of the time
where the time goes in v4:
time: 156 us; the launch traced here: 155 us
  Pallas kernels  147 us (94%)
  local copies, waits for them, and re-layouts  5.76 us (4%)
  other arithmetic  1.75 us (1%)
    pallas_call x1, Pallas kernels, local(): pl.pallas_call(functools.partial(kernel, ny, nx, ranks), in_specs=[smem,...  146 us
    unnamed x18, local copies, waits for them, and re-layouts  5.08 us

profile of v4, /device:TPU:8, one launch (start us, length us, event | category | flops | bytes accessed | tf_op | source)
XLA Modules:
  0.0 155.5 jit_solution(4973491329277019324)
XLA Ops:
  0.6 0.0 copy-start.7
  0.7 0.0 copy-start.8
  0.7 0.0 copy-start.4
  0.7 0.6 copy-done.7
  1.3 0.0 copy-done.8
  1.3 0.0 copy-start.5
  1.3 0.0 copy-start.6
  1.3 0.6 copy-done.5
  2.0 0.0 copy-done.6
  2.0 0.2 fusion.1
  2.2 0.0 copy-done.4
  2.2 0.1 compare_reduce_fusion
  2.3 0.1 iota_compare_fusion
  2.3 0.2 and_reduce_fusion
  2.5 0.6 select_reduce_fusion
  3.1 146.2 %shard_map.128 = (bf16[1,256,256]{2,1,0:T(8,128)(2,1)}, bf16[1,256,256]{2,1,0:T(8,128)(2,1)}, bf16[4,192,256]{2,1,0:T(8,128)(2,1)}, bf16[4,192,256]{2,1,0:T(8,128)(2,1)}, f32[8,128]{1,0:T(8,128)}) custom-call(s32[32]{0:T(128)} %get-tuple-element.26.slot_ref, s32[32]{0:T(128)} %get-tuple-element.25.len_ref, bf16[1,256,256]{2,1,0:T(8,128)(2,1)} %q_ref.1, ...), custom_call_target="tpu_custom_call" | custom-call | tf_op jit(solution)/shard_map/pallas_call | solution.py:429
  149.3 0.0 copy-start
  149.3 1.0 copy-done
  150.3 0.0 copy-start.1
  150.3 1.0 copy-done.1
  151.3 0.0 copy-start.2
  151.3 0.9 copy-done.2
  152.2 0.0 copy-start.3
  152.2 0.9 copy-done.3
  153.1 1.0 shard_map.129
  154.2 0.7 slice_bitcast_fusion
  154.8 0.6 multiply_reduce_fusion
  (2 shorter events, 0.0 us)
Async XLA Ops:
  0.6 0.7 copy-start.7
  0.7 0.7 copy-start.8
  0.7 1.5 copy-start.4
  1.3 0.7 copy-start.5
  1.3 0.7 copy-start.6
  149.3 1.0 copy-start
  150.3 1.0 copy-start.1
  151.3 0.9 copy-start.2
  152.2 0.9 copy-start.3

commit v5 on v4

--- a/solution.py
+++ b/solution.py
@@ -11,7 +11,7 @@
 SCALE = 0.125
 NEG = -1e30
 NX = 4
-LAG = 2
+LAG = 3
 STEPS = ((1, 0), (-1, 0), (0, 1), (0, -1))
 
 
@@ -118,8 +118,9 @@
 
 
 def kernel(
-    ny, nx, ranks, slot_ref, len_ref, q_ref, g_ref, k_ref, v_ref,
-    ctx_ref, gq_ref, dk_ref, dv_ref, mass_ref,
+    ny, nx, ranks, ids_ref, store_ref, length_ref, q_ref, g_ref, k_ref, v_ref,
+    ctx_ref, gq_ref, dk_ref, dv_ref, rel_ref,
+    slot_ref, len_ref,
     aq, ag, km, vm, kt, vt, st, got_x, mid, got_y, fin_x, fin, mass_own, mass_got,
     own_o, own_q, sent_buf, got_buf, dk_acc, dv_acc,
     send_sem, recv_sem, sx_sem, rx_sem, sy_sem, ry_sem, sf_sem, rf_sem, sd_sem, rd_sem, sm_sem, rm_sem, sr_sem, rr_sem,
@@ -228,6 +229,9 @@
 
     live_row = lax.broadcasted_iota(jnp.int32, (rows, target), 0)
 
+    own = lax.axis_index("dp")
+    lane_one = lax.broadcasted_iota(jnp.int32, (1, 128), 1)
+
     def pass_one(i, carry):
         passed = LAG
         for c in range(1, count):
@@ -243,8 +247,21 @@
                     stat_x(c - 1).start()
 
             passed = upto
-        slot = slot_ref[i]
-        live = live_row < len_ref[i]
+        dy = dx = 0
+        for c in range(1, count):
+            dy = jnp.where(i == c, order[c][0], dy)
+            dx = jnp.where(i == c, order[c][1], dx)
+        question = ((own // nx + dy) % ny) * nx + (own % nx + dx) % nx
+        slot = live_len = 0
+        for n in range(ids_ref.shape[1]):
+            passage = ids_ref[question, n]
+            near = store_ref[passage] - own * held
+            mine = (near >= 0) & (near < held)
+            slot += jnp.where(mine, near, 0)
+            live_len += jnp.where(mine, length_ref[passage], 0)
+        slot_ref[i] = slot
+        len_ref[i] = live_len
+        live = live_row < live_len
         all_scores = dot_nt(km[slot], aq[i])
         all_grads = dot_nt(vm[slot], ag[i])
         for h in range(heads):
@@ -369,7 +386,15 @@
     for r in range(1, ranks):
         masses(r).wait_recv()
         mass = mass + mass_got[r]
-    mass_ref[...] = (mass / (target * heads * ranks)).astype(jnp.bfloat16).astype(jnp.float32)
+    mass = (mass / (target * heads * ranks)).astype(jnp.bfloat16).astype(jnp.float32)[:1]
+    place = jnp.full((1, 128), held, jnp.int32)
+    for i in range(count):
+        place = jnp.where(lane_one == i, jnp.where(len_ref[i] > 0, slot_ref[i], held), place)
+    relevance = jnp.zeros((1, 128), jnp.float32)
+    for s in range(held):
+        received = jnp.sum(jnp.where(place == s, mass, 0.0), axis=1, keepdims=True)
+        relevance = jnp.where(lane_one == s, received, relevance)
+    rel_ref[...] = jnp.broadcast_to(relevance, rel_ref.shape)
 
     for g in range(length):
         for copy in gathers(g):
@@ -395,7 +420,6 @@
 
 
 def local(queries, keys, values, cotangent, passage_ids, store_slot, lengths):
-    own = lax.axis_index("dp")
     count = lax.axis_size("dp")
     nx = NX
     ny = count // nx
@@ -405,19 +429,6 @@
     target = queries.shape[1]
     heads = feats // HD
 
-    dys = jnp.array([p[0] for p in order], jnp.int32)
-    dxs = jnp.array([p[1] for p in order], jnp.int32)
-    question = ((own // nx + dys) % ny) * nx + (own % nx + dxs) % nx
-    places = own * held + jnp.arange(held, dtype=jnp.int32)
-    match = (store_slot[None, :] == places[:, None]).astype(jnp.int32)
-    held_id = jnp.sum(match * jnp.arange(store_slot.shape[0], dtype=jnp.int32)[None, :], axis=1)
-    held_len = jnp.sum(match * lengths[None, :], axis=1)
-    hit = jnp.any(passage_ids[:, :, None] == held_id[None, None, :], axis=1)
-    turn = question[:, None] == jnp.arange(count, dtype=jnp.int32)[None, :]
-    used = jnp.any(turn[:, :, None] & hit[None, :, :], axis=1).astype(jnp.int32)
-    slot = jnp.sum(used * jnp.arange(held, dtype=jnp.int32)[None, :], axis=1)
-    live_len = jnp.sum(used * held_len[None, :], axis=1)
-
     vmem = pl.BlockSpec(memory_space=pltpu.VMEM)
     smem = pl.BlockSpec(memory_space=pltpu.SMEM)
     dma = pltpu.SemaphoreType.DMA
@@ -426,12 +437,14 @@
     heads = feats // HD
     lines = heads * target // 128
     outs = [jax.ShapeDtypeStruct(a.shape, a.dtype) for a in (queries, queries, keys, values)]
-    *results, mass = pl.pallas_call(
+    *results, received = pl.pallas_call(
         functools.partial(kernel, ny, nx, ranks),
-        in_specs=[smem, smem] + [vmem] * 4,
+        in_specs=[smem] * 3 + [vmem] * 4,
         out_specs=[vmem] * 5,
         out_shape=outs + [jax.ShapeDtypeStruct((8, 128), full)],
         scratch_shapes=[
+            pltpu.SMEM((count,), jnp.int32),
+            pltpu.SMEM((count,), jnp.int32),
             pltpu.VMEM((count, target, feats), low),
             pltpu.VMEM((count, target, feats), low),
             pltpu.VMEM((held, heads * rows, feats), low),
@@ -462,16 +475,15 @@
         + [dma((ranks,))] * 2
         + [dma((entry_count,))] * 2,
         compiler_params=pltpu.CompilerParams(collective_id=0, has_side_effects=True, vmem_limit_bytes=62 << 20),
-    )(slot, live_len, queries, cotangent, keys, values)
+    )(passage_ids, store_slot, lengths, queries, cotangent, keys, values)
     context, grad_queries, grad_keys, grad_values = pl.pallas_call(
         hand_over,
         in_specs=[vmem] * 4,
         out_specs=[vmem] * 4,
         out_shape=outs,
-        compiler_params=pltpu.CompilerParams(vmem_limit_bytes=16 << 20),
+        compiler_params=pltpu.CompilerParams(vmem_limit_bytes=60 << 20),
     )(*results)
-    relevance = jnp.sum(used.astype(full) * mass[0, :count, None], axis=0)
-    return context, grad_queries, grad_keys, grad_values, relevance
+    return context, grad_queries, grad_keys, grad_values, received[0, :held]
 
 
 def solution(mesh):

time: 156 us -> 149 us (0.955)
  the two profiles are of different devices: /device:TPU:8 before, /device:TPU:16 now
where the time goes in v5:
time: 149 us; the launch traced here: 148 us
  Pallas kernels  145 us (97%)
  local copies, waits for them, and re-layouts  2.56 us (2%)
    pallas_call x1, Pallas kernels, local(): pl.pallas_call(functools.partial(kernel, ny, nx, ranks), in_specs=[smem]...  143 us

profile of v5, /device:TPU:16, one launch (start us, length us, event | category | flops | bytes accessed | tf_op | source)
XLA Modules:
  0.0 148.4 jit_solution(16670767369776859016)
XLA Ops:
  0.6 1.4 copy.12.ids_ref
  2.0 143.0 %shard_map.110 = (bf16[1,256,256]{2,1,0:T(8,128)(2,1)}, bf16[1,256,256]{2,1,0:T(8,128)(2,1)}, bf16[4,192,256]{2,1,0:T(8,128)(2,1)}, bf16[4,192,256]{2,1,0:T(8,128)(2,1)}, f32[8,128]{1,0:T(8,128)}) custom-call(s32[32,16]{1,0:T(8,128)} %copy.12.ids_ref, s32[128]{0:T(128)} %store_ref.1, s32[128]{0:T(128)} %length_ref.1, bf16[1,256,256]{2,1,0:T(8,128)(2,1)} %q_ref.1, ...), custom_call_target="tpu_custom_call" | custom-call | tf_op jit(solution)/shard_map/pallas_call | solution.py:440
  145.0 2.2 %shard_map.111 = (bf16[1,256,256]{2,1,0:T(8,128)(2,1)}, bf16[1,256,256]{2,1,0:T(8,128)(2,1)}, bf16[4,192,256]{2,1,0:T(8,128)(2,1)}, bf16[4,192,256]{2,1,0:T(8,128)(2,1)}) custom-call(bf16[1,256,256]{2,1,0:T(8,128)(2,1)} %get-tuple-element.14.refs_0_, bf16[1,256,256]{2,1,0:T(8,128)(2,1)} %get-tuple-element.15.refs_1_, ...), custom_call_target="tpu_custom_call" | custom-call | tf_op jit(solution)/shard_map/pallas_call | solution.py:479
  147.2 1.2 slice_bitcast_fusion
